TPU v7x, 32 devices: a whole 2x2x4 slice. The times are simulated.
32 devices in a mesh: frame: 8 (over z, y), head: 4 (over x, core).
Axes of the slice: x: 2, y: 2, z: 4, core: 2. Of those that a mesh axis runs over, the one named last changes fastest.
Arguments:
- q_raw: bfloat16 [2, 3072, 5120], P(None, 'frame', 'head'), may hold values from -200 to 200
- k_raw: bfloat16 [2, 3072, 5120], P(None, 'frame', 'head'), may hold values from -200 to 200
- v_in: bfloat16 [2, 3072, 5120], P(None, 'frame', 'head'), may hold values from -6 to 6
- cross_q_raw: bfloat16 [2, 3072, 5120], P(None, 'frame', 'head'), may hold values from -200 to 200
- text_k_raw: bfloat16 [2, 512, 5120], P(None, 'frame', 'head'), may hold values from -200 to 200
- text_v: bfloat16 [2, 512, 5120], P(None, 'frame', 'head'), may hold values from -6 to 6
- q_gain: float32 [5120], P('head'), may hold values from 0.5 to 1.5
- k_gain: float32 [5120], P('head'), may hold values from 0.5 to 1.5
- cross_q_gain: float32 [5120], P('head'), may hold values from 0.5 to 1.5
- text_k_gain: float32 [5120], P('head'), may hold values from 0.5 to 1.5
- nbr: int32 [24, 14], P('frame'), may hold values from 0 to 23, as said below
- nbr_count: int32 [24], P('frame'), may hold values from 7 to 14
- text_len: int32 [2], replicated, may hold values from 256 to 512
Outputs:
- self_out: bfloat16 [2, 3072, 5120], P(None, 'frame', 'head')
- cross_out: bfloat16 [2, 3072, 5120], P(None, 'frame', 'head')
Inputs may be any that keep to these rules, and one draw needn't show every extreme that they name: Row r of nbr begins with r; its first nbr_count[r] entries are distinct tiles whose frame shard (tile // 3) lies at most 2 from that of r; its other entries equal r.
All inputs are finite; a program needn't handle non-finite values.
Results may differ from a plain program's by a relative error of at most 0.002.
The roundings to bfloat16 on the way count: a program that leaves them out, or rounds other values in their place, can miss the bound.
Values may be sent and summed in bfloat16 or wider, within the bound.
No kernel may reach another device: no remote copies, remote signals or barrier semaphores. Data moves between devices by JAX's collectives and lax.ppermute only.
A program may use at most 192 MiB of HBM per device.

v0:
```python
import math

import jax
import jax.numpy as jnp
from jax import lax
from jax.sharding import PartitionSpec as P

D = 5120
HD = 128
NB = 14
REACH = 2


EPSILON = 1e-06


def from_behind(value, axis, by):
    length = lax.axis_size(axis)
    pairs = [(i, i + by) for i in range(length) if 0 <= i + by < length]
    return lax.ppermute(value, axis, pairs)


def squares(tensor):
    values = tensor.astype(jnp.float32)
    return jnp.sum(values * values, axis=-1)


def scaled(tensor, totals, gain_vector):
    factor = lax.rsqrt(totals / D + EPSILON)[..., None]
    return (tensor.astype(jnp.float32) * factor * gain_vector).astype(jnp.bfloat16)


def soft_weights(scores):
    row_top = jnp.max(scores, axis=-1, keepdims=True)
    powers = jnp.exp(scores - row_top)
    return (powers / jnp.sum(powers, axis=-1, keepdims=True)).astype(jnp.bfloat16)


def body(
    q_raw,
    k_raw,
    v_in,
    cross_q_raw,
    text_k_raw,
    text_v,
    q_gain,
    k_gain,
    cross_q_gain,
    text_k_gain,
    nbr,
    nbr_count,
    text_len,
):
    feature_width = q_raw.shape[-1]
    groups = feature_width // HD
    tok_dev = q_raw.shape[1]
    tiles_dev = nbr.shape[0]
    tile_len = tok_dev // tiles_dev
    score_scale = 1.0 / math.sqrt(HD)
    q_total, k_total, cross_total, text_total = lax.psum(
        (squares(q_raw), squares(k_raw), squares(cross_q_raw), squares(text_k_raw)), "head"
    )
    text_local = scaled(text_k_raw, text_total, text_k_gain)
    text_keys, text_values = (
        lax.all_gather(text_local, "frame", axis=1, tiled=True),
        lax.all_gather(text_v, "frame", axis=1, tiled=True),
    )
    queries = scaled(q_raw, q_total, q_gain)
    keys_own = scaled(k_raw, k_total, k_gain)
    cross_queries = scaled(cross_q_raw, cross_total, cross_q_gain)
    pieces = {0: (keys_own, v_in)}
    for offset in range(-REACH, REACH + 1):
        if offset != 0:
            pieces[offset] = from_behind((keys_own, v_in), "frame", -offset)
    ordered = list(range(-REACH, REACH + 1))
    key_buffer = jnp.concatenate([pieces[offset][0] for offset in ordered], axis=1)
    value_buffer = jnp.concatenate([pieces[offset][1] for offset in ordered], axis=1)
    slots_total = (2 * REACH + 1) * tiles_dev
    key_tiles = key_buffer.reshape(2, slots_total, tile_len, feature_width)
    value_tiles = value_buffer.reshape(2, slots_total, tile_len, feature_width)
    first_tile = (lax.axis_index("frame") - REACH) * tiles_dev
    local_index = jnp.clip(nbr - first_tile, 0, slots_total - 1)
    text_total_len = text_keys.shape[1]
    text_heads = text_keys.reshape(2, text_total_len, groups, HD)
    text_value_heads = text_values.reshape(2, text_total_len, groups, HD)
    text_mask = jnp.arange(text_total_len, dtype=jnp.int32)[None, :] < text_len[:, None]
    slot_tile = jnp.arange(NB * tile_len, dtype=jnp.int32) // tile_len

    def one_tile(tile_index):
        row_start = tile_index * tile_len
        slot_list = lax.dynamic_index_in_dim(local_index, tile_index, 0, keepdims=False)
        live_total = lax.dynamic_index_in_dim(nbr_count, tile_index, 0, keepdims=False)
        chosen_keys = jnp.take(key_tiles, slot_list, axis=1).reshape(2, NB * tile_len, groups, HD)
        chosen_values = jnp.take(value_tiles, slot_list, axis=1).reshape(
            2, NB * tile_len, groups, HD
        )
        query_heads = lax.dynamic_slice_in_dim(queries, row_start, tile_len, 1).reshape(
            2, tile_len, groups, HD
        )
        self_scores = (
            jnp.einsum(
                "cqhd,ckhd->chqk", query_heads, chosen_keys, preferred_element_type=jnp.float32
            )
            * score_scale
        )
        live_mask = slot_tile < live_total
        self_scores = jnp.where(live_mask[None, None, None, :], self_scores, -1e30)
        self_weights = soft_weights(self_scores)
        self_rows = jnp.einsum(
            "chqk,ckhd->cqhd", self_weights, chosen_values, preferred_element_type=jnp.float32
        )
        self_rows = self_rows.astype(jnp.bfloat16).reshape(2, tile_len, feature_width)
        cross_heads = lax.dynamic_slice_in_dim(cross_queries, row_start, tile_len, 1).reshape(
            2, tile_len, groups, HD
        )
        cross_scores = (
            jnp.einsum(
                "cqhd,ckhd->chqk", cross_heads, text_heads, preferred_element_type=jnp.float32
            )
            * score_scale
        )
        cross_scores = jnp.where(text_mask[:, None, None, :], cross_scores, -1e30)
        cross_weights = soft_weights(cross_scores)
        cross_rows = jnp.einsum(
            "chqk,ckhd->cqhd", cross_weights, text_value_heads, preferred_element_type=jnp.float32
        )
        cross_rows = cross_rows.astype(jnp.bfloat16).reshape(2, tile_len, feature_width)
        return (self_rows, cross_rows)

    self_tiles, cross_tiles = lax.map(one_tile, jnp.arange(tiles_dev, dtype=jnp.int32))
    self_out = jnp.transpose(self_tiles, (1, 0, 2, 3)).reshape(2, tok_dev, feature_width)
    cross_out = jnp.transpose(cross_tiles, (1, 0, 2, 3)).reshape(2, tok_dev, feature_width)
    return (self_out, cross_out)


def solution(mesh):
    in_specs = (
        P(None, "frame", "head"),
        P(None, "frame", "head"),
        P(None, "frame", "head"),
        P(None, "frame", "head"),
        P(None, "frame", "head"),
        P(None, "frame", "head"),
        P("head"),
        P("head"),
        P("head"),
        P("head"),
        P("frame", None),
        P("frame"),
        P(),
    )
    out_specs = (P(None, "frame", "head"), P(None, "frame", "head"))
    return jax.shard_map(body, mesh=mesh, in_specs=in_specs, out_specs=out_specs, check_vma=False)
```

profile of v0, /device:TPU:0, one launch (start us, length us, event | category | flops | bytes accessed | tf_op | source)
XLA Modules:
  0.0 800.4 jit_solution(1656501868277427561)
XLA Ops:
  7.2 4.0 copy.48
  13.3 4.0 copy.49
  20.0 12.6 %all-reduce = (f32[2,384]{1,0:T(2,128)S(1)}, f32[2,384]{1,0:T(2,128)S(1)}, f32[2,384]{1,0:T(2,128)S(1)}, f32[2,64]{1,0:T(2,128)S(1)}) all-reduce(f32[2,384]{1,0:T(2,128)S(1)} %fusion.31, f32[2,384]{1,0:T(2,128)S(1)} %fusion.34, f32[2,384]{1,0:T(2,128)S(1)} %fusion.37, ...), channel_id=1, replica_groups=mesh['frame'=8,'head'=4] {'head'}, use_global_device_ids=true, to_apply=%region_3.0 | all-reduce | flops 2432 | bytes 19456 | tf_op jit(solution)/shard_map/psum | solution.py:60
  33.9 4.8 collective-permute-start
  40.5 3.5 collective-permute-start.4
  44.0 4.7 collective-permute-start.5
  50.0 5.8 collective-permute-start.1
  62.6 46.8 %collective-permute-done = bf16[2,384,1280]{2,1,0:T(8,128)(2,1)} collective-permute-done((bf16[2,384,1280]{2,1,0:T(8,128)(2,1)}, bf16[2,384,1280]{2,1,0:T(8,128)(2,1)}, u32[]{:S(2)}, u32[]{:S(2)}) %collective-permute-start) | collective-permute-done | bytes 1966112 | tf_op jit(solution)/shard_map/ppermute | solution.py:20
  113.6 88.8 %collective-permute-done.1 = bf16[2,384,1280]{2,1,0:T(8,128)(2,1)} collective-permute-done((bf16[2,384,1280]{2,1,0:T(8,128)(2,1)}, bf16[2,384,1280]{2,1,0:T(8,128)(2,1)}, u32[]{:S(2)}, u32[]{:S(2)}) %collective-permute-start.1) | collective-permute-done | bytes 1966112 | tf_op jit(solution)/shard_map/ppermute | solution.py:20
  223.0 88.9 %collective-permute-done.2 = bf16[2,384,1280]{2,1,0:T(8,128)(2,1)S(1)} collective-permute-done((bf16[2,384,1280]{2,1,0:T(8,128)(2,1)}, bf16[2,384,1280]{2,1,0:T(8,128)(2,1)S(1)}, u32[]{:S(2)}, u32[]{:S(2)}) %collective-permute-start.2) | collective-permute-done | bytes 1966112 | tf_op jit(solution)/shard_map/ppermute | solution.py:20
  313.3 42.6 %collective-permute-done.3 = bf16[2,384,1280]{2,1,0:T(8,128)(2,1)S(1)} collective-permute-done((bf16[2,384,1280]{2,1,0:T(8,128)(2,1)}, bf16[2,384,1280]{2,1,0:T(8,128)(2,1)S(1)}, u32[]{:S(2)}, u32[]{:S(2)}) %collective-permute-start.3) | collective-permute-done | bytes 1966112 | tf_op jit(solution)/shard_map/ppermute | solution.py:20
  357.3 5.9 copy.51
  365.8 4.5 copy.52
  370.4 416.9 %while.13 = (s32[]{:T(128)}, bf16[3,2,128,1280]{2,3,1,0:T(8,128)(2,1)S(1)}, bf16[3,2,128,1280]{2,3,1,0:T(8,128)(2,1)}, s32[3]{0:T(128)S(1)}, s32[3,14]{1,0:T(4,1...) while((s32[]{:T(128)}, ...), condition=%wide.region_13.15_spmd.clone, body=%wide.region_8.14_spmd.clone.sunk | while | flops 3065139200 | bytes 225495648 | solution.py:130
  373.2 9.1 %gather_fusion = bf16[14,2,128,1280]{3,2,1,0:T(8,128)(2,1)} fusion(bf16[2,15,128,1280]{3,2,1,0:T(8,128)(2,1)} %get-tuple-element.332, s32[1024]{0:T(1024)S(1)} %pad_clamp_fusion.2), kind=kCustom, calls=%fused_computation.1.clone.clone.1 | custom fusion | bytes 18350136 | tf_op jit(solution)/shard_map/while/body/eval_jaxpr/jit(_take)/gather | solution.py:93
  382.2 9.0 %gather_fusion.1 = bf16[14,2,128,1280]{3,2,1,0:T(8,128)(2,1)} fusion(bf16[2,15,128,1280]{3,2,1,0:T(8,128)(2,1)} %get-tuple-element.329, s32[1024]{0:T(1024)S(1)} %pad_clamp_fusion.2), kind=kCustom, calls=%fused_computation.clone.clone.1 | custom fusion | bytes 18350136 | tf_op jit(solution)/shard_map/while/body/eval_jaxpr/jit(_take)/gather | solution.py:94
  391.2 14.9 %select_bitcast_fusion.3 = (bf16[2,14,128,1280]{3,2,0,1:T(8,128)(2,1)}, bf16[2,14,128,1280]{3,2,0,1:T(8,128)(2,1)}) fusion(bf16[14,2,128,1280]{3,2,1,0:T(8,128)(2,1)} %gather_fusion, pred[14]{0:T(512)(128)(4,1)S(1)} %get-tuple-element.281, bf16[14,2,128,1280]{3,2,1,0:T(8,128)(2,1)} %gather_fusion.1), kind=kLoop, calls=%fused_computation.10.clone.1 | loop fusion | flops 9175040 | bytes 36700176 | tf_op jit(solution)/shard_map/while/body/eval_jaxpr/jit(_take)/select_n | solution.py:93
  406.1 15.9 %copy.62 = bf16[2,14,128,1280]{2,1,3,0:T(8,128)(2,1)} copy(bf16[2,14,128,1280]{3,2,0,1:T(8,128)(2,1)} %get-tuple-element.283) | data formatting | bytes 18350080 | tf_op jit(solution)/shard_map/while/body/eval_jaxpr/jit(_take)/select_n | solution.py:93
  422.0 16.3 %reshape.103 = bf16[2,1792,10,128]{1,3,2,0:T(8,128)(2,1)} reshape(bf16[2,14,128,1280]{2,1,3,0:T(8,128)(2,1)} %copy.62) | data formatting | bytes 18350080 | tf_op jit(solution)/shard_map/while/body/eval_jaxpr/reshape | solution.py:93
  441.3 12.3 %fusion.75 = (f32[2,10,128]{2,1,0:T(8,128)S(1)}, f32[2,10,128,1792]{3,2,1,0:T(8,128)}) fusion(pred[1792]{0:T(1024)(128)(4,1)S(1)} %fusion.74, bf16[2,128,10,128]{1,3,2,0:T(8,128)(2,1)S(1)} %bitcast.67, bf16[2,1792,10,128]{1,3,2,0:T(8,128)(2,1)} %reshape.103), kind=kOutput, calls=%fused_computation.85.clone.1 | convolution fusion | flops 1192756992 | bytes 28192512 | tf_op jit(solution)/shard_map/while/body/eval_jaxpr/sub | solution.py:35
  453.6 16.0 %copy.61 = bf16[2,14,128,1280]{2,1,3,0:T(8,128)(2,1)} copy(bf16[2,14,128,1280]{3,2,0,1:T(8,128)(2,1)} %get-tuple-element.282) | data formatting | bytes 18350080 | tf_op jit(solution)/shard_map/while/body/eval_jaxpr/jit(_take)/select_n | solution.py:94
  469.5 16.2 %reshape.102 = bf16[2,1792,10,128]{1,3,2,0:T(8,128)(2,1)} reshape(bf16[2,14,128,1280]{2,1,3,0:T(8,128)(2,1)} %copy.61) | data formatting | bytes 18350080 | tf_op jit(solution)/shard_map/while/body/eval_jaxpr/reshape | solution.py:94
  485.7 11.4 %fusion.76 = bf16[2,10,128,128]{3,2,1,0:T(8,128)(2,1)S(1)} fusion(bf16[2,1792,10,128]{1,3,2,0:T(8,128)(2,1)} %reshape.102, f32[2,10,128,1792]{3,2,1,0:T(8,128)} %get-tuple-element.284, f32[2,10,128]{2,1,0:T(8,128)S(1)} %get-tuple-element.285), kind=kOutput, calls=%fused_computation.25.clone.1 | convolution fusion | flops 1183907840 | bytes 28190720 | tf_op jit(solution)/shard_map/while/body/eval_jaxpr/chqk,ckhd->cqhd/dot_general | solution.py:109
  498.4 5.8 fusion.72
  504.2 4.3 fusion.73
  512.0 9.1 %gather_fusion = bf16[14,2,128,1280]{3,2,1,0:T(8,128)(2,1)} fusion(bf16[2,15,128,1280]{3,2,1,0:T(8,128)(2,1)} %get-tuple-element.332, s32[1024]{0:T(1024)S(1)} %pad_clamp_fusion.2), kind=kCustom, calls=%fused_computation.1.clone.clone.1 | custom fusion | bytes 18350136 | tf_op jit(solution)/shard_map/while/body/eval_jaxpr/jit(_take)/gather | solution.py:93
  521.1 9.0 %gather_fusion.1 = bf16[14,2,128,1280]{3,2,1,0:T(8,128)(2,1)} fusion(bf16[2,15,128,1280]{3,2,1,0:T(8,128)(2,1)} %get-tuple-element.329, s32[1024]{0:T(1024)S(1)} %pad_clamp_fusion.2), kind=kCustom, calls=%fused_computation.clone.clone.1 | custom fusion | bytes 18350136 | tf_op jit(solution)/shard_map/while/body/eval_jaxpr/jit(_take)/gather | solution.py:94
  530.1 14.9 %select_bitcast_fusion.3 = (bf16[2,14,128,1280]{3,2,0,1:T(8,128)(2,1)}, bf16[2,14,128,1280]{3,2,0,1:T(8,128)(2,1)}) fusion(bf16[14,2,128,1280]{3,2,1,0:T(8,128)(2,1)} %gather_fusion, pred[14]{0:T(512)(128)(4,1)S(1)} %get-tuple-element.281, bf16[14,2,128,1280]{3,2,1,0:T(8,128)(2,1)} %gather_fusion.1), kind=kLoop, calls=%fused_computation.10.clone.1 | loop fusion | flops 9175040 | bytes 36700176 | tf_op jit(solution)/shard_map/while/body/eval_jaxpr/jit(_take)/select_n | solution.py:93
  545.0 15.9 %copy.62 = bf16[2,14,128,1280]{2,1,3,0:T(8,128)(2,1)} copy(bf16[2,14,128,1280]{3,2,0,1:T(8,128)(2,1)} %get-tuple-element.283) | data formatting | bytes 18350080 | tf_op jit(solution)/shard_map/while/body/eval_jaxpr/jit(_take)/select_n | solution.py:93
  560.9 16.3 %reshape.103 = bf16[2,1792,10,128]{1,3,2,0:T(8,128)(2,1)} reshape(bf16[2,14,128,1280]{2,1,3,0:T(8,128)(2,1)} %copy.62) | data formatting | bytes 18350080 | tf_op jit(solution)/shard_map/while/body/eval_jaxpr/reshape | solution.py:93
  580.3 12.3 %fusion.75 = (f32[2,10,128]{2,1,0:T(8,128)S(1)}, f32[2,10,128,1792]{3,2,1,0:T(8,128)}) fusion(pred[1792]{0:T(1024)(128)(4,1)S(1)} %fusion.74, bf16[2,128,10,128]{1,3,2,0:T(8,128)(2,1)S(1)} %bitcast.67, bf16[2,1792,10,128]{1,3,2,0:T(8,128)(2,1)} %reshape.103), kind=kOutput, calls=%fused_computation.85.clone.1 | convolution fusion | flops 1192756992 | bytes 28192512 | tf_op jit(solution)/shard_map/while/body/eval_jaxpr/sub | solution.py:35
  592.5 16.0 %copy.61 = bf16[2,14,128,1280]{2,1,3,0:T(8,128)(2,1)} copy(bf16[2,14,128,1280]{3,2,0,1:T(8,128)(2,1)} %get-tuple-element.282) | data formatting | bytes 18350080 | tf_op jit(solution)/shard_map/while/body/eval_jaxpr/jit(_take)/select_n | solution.py:94
  608.5 16.2 %reshape.102 = bf16[2,1792,10,128]{1,3,2,0:T(8,128)(2,1)} reshape(bf16[2,14,128,1280]{2,1,3,0:T(8,128)(2,1)} %copy.61) | data formatting | bytes 18350080 | tf_op jit(solution)/shard_map/while/body/eval_jaxpr/reshape | solution.py:94
  624.7 11.4 %fusion.76 = bf16[2,10,128,128]{3,2,1,0:T(8,128)(2,1)S(1)} fusion(bf16[2,1792,10,128]{1,3,2,0:T(8,128)(2,1)} %reshape.102, f32[2,10,128,1792]{3,2,1,0:T(8,128)} %get-tuple-element.284, f32[2,10,128]{2,1,0:T(8,128)S(1)} %get-tuple-element.285), kind=kOutput, calls=%fused_computation.25.clone.1 | convolution fusion | flops 1183907840 | bytes 28190720 | tf_op jit(solution)/shard_map/while/body/eval_jaxpr/chqk,ckhd->cqhd/dot_general | solution.py:109
  637.4 5.8 fusion.72
  643.2 4.2 fusion.73
  650.9 9.1 %gather_fusion = bf16[14,2,128,1280]{3,2,1,0:T(8,128)(2,1)} fusion(bf16[2,15,128,1280]{3,2,1,0:T(8,128)(2,1)} %get-tuple-element.332, s32[1024]{0:T(1024)S(1)} %pad_clamp_fusion.2), kind=kCustom, calls=%fused_computation.1.clone.clone.1 | custom fusion | bytes 18350136 | tf_op jit(solution)/shard_map/while/body/eval_jaxpr/jit(_take)/gather | solution.py:93
  660.1 9.0 %gather_fusion.1 = bf16[14,2,128,1280]{3,2,1,0:T(8,128)(2,1)} fusion(bf16[2,15,128,1280]{3,2,1,0:T(8,128)(2,1)} %get-tuple-element.329, s32[1024]{0:T(1024)S(1)} %pad_clamp_fusion.2), kind=kCustom, calls=%fused_computation.clone.clone.1 | custom fusion | bytes 18350136 | tf_op jit(solution)/shard_map/while/body/eval_jaxpr/jit(_take)/gather | solution.py:94
  669.1 14.9 %select_bitcast_fusion.3 = (bf16[2,14,128,1280]{3,2,0,1:T(8,128)(2,1)}, bf16[2,14,128,1280]{3,2,0,1:T(8,128)(2,1)}) fusion(bf16[14,2,128,1280]{3,2,1,0:T(8,128)(2,1)} %gather_fusion, pred[14]{0:T(512)(128)(4,1)S(1)} %get-tuple-element.281, bf16[14,2,128,1280]{3,2,1,0:T(8,128)(2,1)} %gather_fusion.1), kind=kLoop, calls=%fused_computation.10.clone.1 | loop fusion | flops 9175040 | bytes 36700176 | tf_op jit(solution)/shard_map/while/body/eval_jaxpr/jit(_take)/select_n | solution.py:93
  684.0 15.9 %copy.62 = bf16[2,14,128,1280]{2,1,3,0:T(8,128)(2,1)} copy(bf16[2,14,128,1280]{3,2,0,1:T(8,128)(2,1)} %get-tuple-element.283) | data formatting | bytes 18350080 | tf_op jit(solution)/shard_map/while/body/eval_jaxpr/jit(_take)/select_n | solution.py:93
  699.8 16.3 %reshape.103 = bf16[2,1792,10,128]{1,3,2,0:T(8,128)(2,1)} reshape(bf16[2,14,128,1280]{2,1,3,0:T(8,128)(2,1)} %copy.62) | data formatting | bytes 18350080 | tf_op jit(solution)/shard_map/while/body/eval_jaxpr/reshape | solution.py:93
  719.2 12.3 %fusion.75 = (f32[2,10,128]{2,1,0:T(8,128)S(1)}, f32[2,10,128,1792]{3,2,1,0:T(8,128)}) fusion(pred[1792]{0:T(1024)(128)(4,1)S(1)} %fusion.74, bf16[2,128,10,128]{1,3,2,0:T(8,128)(2,1)S(1)} %bitcast.67, bf16[2,1792,10,128]{1,3,2,0:T(8,128)(2,1)} %reshape.103), kind=kOutput, calls=%fused_computation.85.clone.1 | convolution fusion | flops 1192756992 | bytes 28192512 | tf_op jit(solution)/shard_map/while/body/eval_jaxpr/sub | solution.py:35
  731.4 16.0 %copy.61 = bf16[2,14,128,1280]{2,1,3,0:T(8,128)(2,1)} copy(bf16[2,14,128,1280]{3,2,0,1:T(8,128)(2,1)} %get-tuple-element.282) | data formatting | bytes 18350080 | tf_op jit(solution)/shard_map/while/body/eval_jaxpr/jit(_take)/select_n | solution.py:94
  747.4 16.2 %reshape.102 = bf16[2,1792,10,128]{1,3,2,0:T(8,128)(2,1)} reshape(bf16[2,14,128,1280]{2,1,3,0:T(8,128)(2,1)} %copy.61) | data formatting | bytes 18350080 | tf_op jit(solution)/shard_map/while/body/eval_jaxpr/reshape | solution.py:94
  763.6 11.4 %fusion.76 = bf16[2,10,128,128]{3,2,1,0:T(8,128)(2,1)S(1)} fusion(bf16[2,1792,10,128]{1,3,2,0:T(8,128)(2,1)} %reshape.102, f32[2,10,128,1792]{3,2,1,0:T(8,128)} %get-tuple-element.284, f32[2,10,128]{2,1,0:T(8,128)S(1)} %get-tuple-element.285), kind=kOutput, calls=%fused_computation.25.clone.1 | convolution fusion | flops 1183907840 | bytes 28190720 | tf_op jit(solution)/shard_map/while/body/eval_jaxpr/chqk,ckhd->cqhd/dot_general | solution.py:109
  776.3 5.8 fusion.72
  782.1 4.3 fusion.73
  789.6 4.0 copy.55
  (89 shorter events, 63.8 us)
Async XLA Ops:
  7.2 350.2 %all-gather.3.cloned.1.call-start = ((), (), s32[]{:S(2)}) async-start(), calls=%async_computation | async-start | bytes 2949120 | tf_op jit(solution)/shard_map/all_gather | solution.py:65
  11.2 8.1 %copy-start = (bf16[2,384,1280]{2,1,0:T(8,128)(2,1)S(1)}, bf16[2,384,1280]{2,1,0:T(8,128)(2,1)}, u32[]{:S(2)}) copy-start(bf16[2,384,1280]{2,1,0:T(8,128)(2,1)} %param.18) | copy-start | bytes 5898244
  13.3 6.5 copy-start.2
  13.3 19.3 %copy-start.7 = (f32[1280]{0:T(1024)S(1)}, f32[1280]{0:T(1024)}, u32[]{:S(2)}) copy-start(f32[1280]{0:T(1024)} %param.26) | copy-start | bytes 15364
  17.3 21.4 %copy-start.3 = (f32[1280]{0:T(1024)S(1)}, f32[1280]{0:T(1024)}, u32[]{:S(2)}) copy-start(f32[1280]{0:T(1024)} %param.24) | copy-start | bytes 15364
  19.3 36.5 %copy-start.5 = (f32[1280]{0:T(1024)S(1)}, f32[1280]{0:T(1024)}, u32[]{:S(2)}) copy-start(f32[1280]{0:T(1024)} %param.23) | copy-start | bytes 15364
  33.8 332.0 %all-gather.5.cloned.1.call-start = ((), (), s32[]{:S(2)}) async-start(), calls=%async_computation.1 | async-start | bytes 2949120 | tf_op jit(solution)/shard_map/all_gather | solution.py:66
  33.9 75.5 %collective-permute-start = (bf16[2,384,1280]{2,1,0:T(8,128)(2,1)}, bf16[2,384,1280]{2,1,0:T(8,128)(2,1)}, u32[]{:S(2)}, u32[]{:S(2)}) collective-permute-start(bf16[2,384,1280]{2,1,0:T(8,128)(2,1)} %param.19), channel_id=1, source_target_pairs={{0,8},{4,12},{8,16},{12,20},{16,24},{20,28},{1,9},{5,13},{9,17},{1... | collective-permute-start | bytes 5898248 | tf_op jit(solution)/shard_map/ppermute | solution.py:20
  38.7 20.5 %copy-start.8 = (s32[3,14]{1,0:T(4,128)S(1)}, s32[3,14]{1,0:T(4,128)}, u32[]{:S(2)}) copy-start(s32[3,14]{1,0:T(4,128)} %param.27) | copy-start | bytes 508
  38.7 20.5 %copy-start.6 = (f32[1280]{0:T(1024)S(1)}, f32[1280]{0:T(1024)}, u32[]{:S(2)}) copy-start(f32[1280]{0:T(1024)} %param.25) | copy-start | bytes 15364
  40.5 169.1 %collective-permute-start.4 = (bf16[2,384,1280]{2,1,0:T(8,128)(2,1)}, bf16[2,384,1280]{2,1,0:T(8,128)(2,1)}, u32[]{:S(2)}, u32[]{:S(2)}) collective-permute-start(bf16[2,384,1280]{2,1,0:T(8,128)(2,1)} %fusion.36), channel_id=1, source_target_pairs={{0,8},{4,12},{8,16},{12,20},{16,24},{20,28},{1,9},{5,13},{9,17},{1... | collective-permute-start | bytes 5898248 | tf_op jit(solution)/shard_map/ppermute | solution.py:20
  44.0 169.9 %collective-permute-start.5 = (bf16[2,384,1280]{2,1,0:T(8,128)(2,1)}, bf16[2,384,1280]{2,1,0:T(8,128)(2,1)}, u32[]{:S(2)}, u32[]{:S(2)}) collective-permute-start(bf16[2,384,1280]{2,1,0:T(8,128)(2,1)} %fusion.36), channel_id=1, source_target_pairs={{0,4},{4,8},{8,12},{12,16},{16,20},{20,24},{24,28},{1,5},{5,9},{9,... | collective-permute-start | bytes 5898248 | tf_op jit(solution)/shard_map/ppermute | solution.py:20
  48.7 169.9 %collective-permute-start.6 = (bf16[2,384,1280]{2,1,0:T(8,128)(2,1)}, bf16[2,384,1280]{2,1,0:T(8,128)(2,1)}, u32[]{:S(2)}, u32[]{:S(2)}) collective-permute-start(bf16[2,384,1280]{2,1,0:T(8,128)(2,1)} %fusion.36), channel_id=1, source_target_pairs={{4,0},{8,4},{12,8},{16,12},{20,16},{24,20},{28,24},{5,1},{9,5},{13... | collective-permute-start | bytes 5898248 | tf_op jit(solution)/shard_map/ppermute | solution.py:20
  50.0 152.4 %collective-permute-start.1 = (bf16[2,384,1280]{2,1,0:T(8,128)(2,1)}, bf16[2,384,1280]{2,1,0:T(8,128)(2,1)}, u32[]{:S(2)}, u32[]{:S(2)}) collective-permute-start(bf16[2,384,1280]{2,1,0:T(8,128)(2,1)} %param.19), channel_id=1, source_target_pairs={{0,4},{4,8},{8,12},{12,16},{16,20},{20,24},{24,28},{1,5},{5,9},{9,... | collective-permute-start | bytes 5898248 | tf_op jit(solution)/shard_map/ppermute | solution.py:20
  109.3 112.3 %collective-permute-start.7 = (bf16[2,384,1280]{2,1,0:T(8,128)(2,1)}, bf16[2,384,1280]{2,1,0:T(8,128)(2,1)S(1)}, u32[]{:S(2)}, u32[]{:S(2)}) collective-permute-start(bf16[2,384,1280]{2,1,0:T(8,128)(2,1)} %fusion.36), channel_id=1, source_target_pairs={{8,0},{12,4},{16,8},{20,12},{24,16},{28,20},{9,1},{13,5},{17,9},{2... | collective-permute-start | bytes 5898248 | tf_op jit(solution)/shard_map/ppermute | solution.py:20
  202.4 109.5 %collective-permute-start.2 = (bf16[2,384,1280]{2,1,0:T(8,128)(2,1)}, bf16[2,384,1280]{2,1,0:T(8,128)(2,1)S(1)}, u32[]{:S(2)}, u32[]{:S(2)}) collective-permute-start(bf16[2,384,1280]{2,1,0:T(8,128)(2,1)} %param.19), channel_id=1, source_target_pairs={{4,0},{8,4},{12,8},{16,12},{20,16},{24,20},{28,24},{5,1},{9,5},{13... | collective-permute-start | bytes 5898248 | tf_op jit(solution)/shard_map/ppermute | solution.py:20
  209.7 146.3 %collective-permute-start.3 = (bf16[2,384,1280]{2,1,0:T(8,128)(2,1)}, bf16[2,384,1280]{2,1,0:T(8,128)(2,1)S(1)}, u32[]{:S(2)}, u32[]{:S(2)}) collective-permute-start(bf16[2,384,1280]{2,1,0:T(8,128)(2,1)} %param.19), channel_id=1, source_target_pairs={{8,0},{12,4},{16,8},{20,12},{24,16},{28,20},{9,1},{13,5},{17,9},{2... | collective-permute-start | bytes 5898248 | tf_op jit(solution)/shard_map/ppermute | solution.py:20
  365.8 4.6 copy-start.1
  365.8 4.6 copy-start.4
  365.8 4.6 copy-start.9
Sparse Core Ops, SparseCore 0:
  33.9 91.6 all-gather.2
  127.9 92.6 all-gather.4
where the time goes:
time: 807 us; the launch traced here: 800 us
  local copies, waits for them, and re-layouts  311 us (39%)
  waiting for transfers between devices  267 us (33%)
  matrix products  101 us (13%)
  other arithmetic  62 us (8%)
  starting transfers between devices  24 us (3%)
  between operations  14.2 us (2%)
  blocking collectives  12.6 us (2%)
  loops' own time  8.14 us (1%)
    ppermute x8, waiting for transfers between devices, from_behind(): return lax.ppermute(value, axis, pairs)  267 us
    sub x6, matrix products, soft_weights(): powers = jnp.exp(scores - row_top)  54.3 us
    reshape x3, local copies, waits for them, and re-layouts, one_tile(): jnp.take(key_tiles, slot_list, axis=1).reshape(2, NB * tile_len, groups, HD)  48.9 us
    reshape x3, local copies, waits for them, and re-layouts, one_tile(): jnp.take(value_tiles, slot_list, axis=1)  48.6 us
    select_n x3, local copies, waits for them, and re-layouts, one_tile(): jnp.take(value_tiles, slot_list, axis=1)  47.9 us
    select_n x3, local copies, waits for them, and re-layouts, one_tile(): jnp.take(key_tiles, slot_list, axis=1).reshape(2, NB * tile_len, groups, HD)  47.6 us
    select_n x3, other arithmetic, one_tile(): jnp.take(key_tiles, slot_list, axis=1).reshape(2, NB * tile_len, groups, HD)  44.7 us
    dot_general x3, matrix products, one_tile(): jnp.einsum('chqk,ckhd->cqhd', self_weights, chosen_values, preferred_elem...  34.3 us
  transfers between devices with their start and end apart: 10, of which 4 were waited for; matrix products, arithmetic and copies ran while one was open for 5% of the time, Pallas kernels for 0%

commit v1 on v0

v1 whole, which is shorter than its diff:
```python
import functools
import math

import jax
import jax.numpy as jnp
from jax import lax
from jax.experimental import pallas as pl
from jax.experimental.pallas import tpu as pltpu
from jax.sharding import PartitionSpec as P

D = 5120
HD = 128
EPSILON = 1e-06
LEAST = 7
FAR = -1e30
SCALE2 = math.log2(math.e) / math.sqrt(HD)
VMEM = 56 * 1024 * 1024
BF = jnp.bfloat16
F32 = jnp.float32


def squares(tensor):
    values = tensor.astype(F32)
    return jnp.sum(values * values, axis=-1)


def weigh(stages, scratch):
    held = {}

    def scores(number):
        top, at, spans = None, 0, []
        for block in stages[number][0]:
            score = block()
            width = score.shape[1]
            scratch[number % 3, :, at : at + width] = score
            spans.append((at, width))
            at += width
            for c in range(0, width, 128):
                part = score[:, c : c + 128]
                top = part if top is None else jnp.maximum(top, part)
        held[number] = spans, jnp.max(top, axis=1, keepdims=True)

    def powers(number):
        spans, top = held[number]
        total = None
        for start, width in spans:
            for c in range(start, start + width, 128):
                power = jnp.exp2((scratch[number % 3, :, c : c + 128] - top) * SCALE2)
                scratch[number % 3, :, c : c + 128] = power
                total = power if total is None else total + power
        held[number] = spans, 1.0 / jnp.sum(total, axis=1, keepdims=True)

    def products(number):
        spans, inverse = held[number]
        out = None
        for (start, width), value in zip(spans, stages[number][1]):
            weights = (scratch[number % 3, :, start : start + width] * inverse).astype(BF)
            part = jnp.dot(weights, value(), preferred_element_type=F32)
            out = part if out is None else out + part
        stages[number][2](out.astype(BF))

    for step in range(len(stages) + 2):
        for work, number in ((scores, step), (powers, step - 1), (products, step - 2)):
            if 0 <= number < len(stages):
                work(number)


def pack_kernel(side, totals, gains, *refs):
    raws, outs = refs[:3], refs[3:]
    rows = raws[0].shape[1]
    width = raws[0].shape[2]

    def write(dest):
        for i in range(3):
            row = totals[0, i, :, :]
            factor = lax.rsqrt(row / D + EPSILON)
            column = jnp.transpose(jnp.broadcast_to(factor, (HD, rows)))
            for c in range(0, width, HD):
                value = raws[i][0, :, c : c + HD].astype(F32)
                dest[i][:, c : c + HD] = (value * column * gains[i : i + 1, c : c + HD]).astype(BF)

    @pl.when(pl.program_id(0) == 0)
    def _():
        write(outs[:3])

    @pl.when(pl.program_id(0) == 1)
    def _():
        write(outs[3:])


def pack(side, totals, gains, raws):
    tokens, width = raws[0].shape[1:]
    rows = 128
    steps = tokens // rows

    raw_spec = pl.BlockSpec((1, rows, width), lambda i, t, side_ref: ((side_ref[0] + i) % 2, t, 0))
    total_spec = pl.BlockSpec(
        (1, 3, 1, rows), lambda i, t, side_ref: ((side_ref[0] + i) % 2, 0, 0, t)
    )
    gain_spec = pl.BlockSpec(gains.shape, lambda i, t, side_ref: (0, 0))
    keep_spec = pl.BlockSpec((rows, width), lambda i, t, side_ref: (t * (1 - i) + (steps - 1) * i, 0))
    send_spec = pl.BlockSpec((rows, width), lambda i, t, side_ref: (t * i, 0))
    return pl.pallas_call(
        pack_kernel,
        grid_spec=pltpu.PrefetchScalarGridSpec(
            num_scalar_prefetch=1,
            grid=(2, steps),
            in_specs=[total_spec, gain_spec] + [raw_spec] * 3,
            out_specs=[keep_spec] * 3 + [send_spec] * 3,
        ),
        out_shape=[jax.ShapeDtypeStruct((tokens, width), BF)] * 6,
        compiler_params=pltpu.CompilerParams(vmem_limit_bytes=VMEM),
        cost_estimate=pl.CostEstimate(
            flops=0, bytes_accessed=12 * tokens * width * 2, transcendentals=0
        ),
        name="norm_pack",
    )(side, totals, gains, *raws)


def join_kernel(first, second, *outs, spans):
    for i, ref in enumerate((first, second)):

        @pl.when(pl.program_id(0) == i)
        def _(ref=ref):
            for out, (c0, c1) in zip(outs, spans):
                out[...] = ref[:, c0:c1]


def join(first, second, spans):
    tokens, width = first.shape
    return pl.pallas_call(
        functools.partial(join_kernel, spans=spans),
        grid=(2,),
        in_specs=[pl.BlockSpec((tokens, width), lambda i: (0, 0))] * 2,
        out_specs=[pl.BlockSpec((tokens, c1 - c0), lambda i: (i, 0)) for c0, c1 in spans],
        out_shape=[jax.ShapeDtypeStruct((2 * tokens, c1 - c0), BF) for c0, c1 in spans],
        compiler_params=pltpu.CompilerParams(vmem_limit_bytes=VMEM),
        cost_estimate=pl.CostEstimate(
            flops=0, bytes_accessed=4 * tokens * width * 2, transcendentals=0
        ),
        name="join",
    )(first, second)


def self_kernel(index, count, *refs, tile, slots, n_k, n_v):
    k_pieces, v_pieces = refs[:n_k], refs[n_k : n_k + n_v]
    q_pieces, out_pieces = refs[n_k + n_v : n_k + n_v + 2], refs[n_k + n_v + 2 : n_k + n_v + 4]
    k_window, v_window, scratch = refs[n_k + n_v + 4 :]
    at = 0
    for piece in k_pieces:
        for start in range(0, piece.shape[0], tile):
            k_window[at] = jnp.transpose(piece[start : start + tile, :])
            at += 1
    at = 0
    for piece in v_pieces:
        for start in range(0, piece.shape[0], tile):
            v_window[at] = piece[start : start + tile, :]
            at += 1
    readers = q_pieces[0].shape[0] // tile
    column = lax.broadcasted_iota(jnp.int32, (1, 2 * tile), 1)

    def stage(half, r):
        number = half * readers + r
        live = count[number]
        rows = slice(r * tile, (r + 1) * tile)

        def block(slot):
            pair = [k_window[index[number * slots + slot + i]] for i in range(2)]
            score = jnp.dot(
                q_pieces[half][rows, :],
                jnp.concatenate(pair, axis=1),
                preferred_element_type=F32,
            )
            if slot + 1 >= LEAST:
                score = jnp.where(column < (live - slot) * tile, score, FAR)
            return score

        def value(slot):
            pair = [v_window[index[number * slots + slot + i]] for i in range(2)]
            return jnp.concatenate(pair, axis=0)

        def store(out):
            out_pieces[half][rows, :] = out

        return (
            [functools.partial(block, slot) for slot in range(0, slots, 2)],
            [functools.partial(value, slot) for slot in range(0, slots, 2)],
            store,
        )

    weigh([stage(half, r) for half in range(2) for r in range(readers)], scratch)


def self_attention(index, count, k_pieces, v_pieces, q_pieces, first_head, tile, slots):
    tokens = q_pieces[0].shape[0]
    width = k_pieces[0].shape[1]
    heads = width // HD
    window = 6 * tokens // tile

    def spec(piece, base):
        return pl.BlockSpec((piece.shape[0], HD), lambda h, *_: (0, h + base))

    rows = 2 * tokens * heads
    return pl.pallas_call(
        functools.partial(
            self_kernel, tile=tile, slots=slots, n_k=len(k_pieces), n_v=len(v_pieces)
        ),
        grid_spec=pltpu.PrefetchScalarGridSpec(
            num_scalar_prefetch=2,
            grid=(heads,),
            in_specs=[spec(piece, 0) for piece in k_pieces]
            + [spec(piece, first_head) for piece in (*v_pieces, *q_pieces)],
            out_specs=[pl.BlockSpec((tokens, HD), lambda h, *_: (0, h))] * 2,
            scratch_shapes=[
                pltpu.VMEM((window, HD, tile), BF),
                pltpu.VMEM((window, tile, HD), BF),
                pltpu.VMEM((3, tile, slots * tile), F32),
            ],
        ),
        out_shape=[jax.ShapeDtypeStruct((tokens, width), BF)] * 2,
        compiler_params=pltpu.CompilerParams(vmem_limit_bytes=VMEM),
        cost_estimate=pl.CostEstimate(
            flops=rows * slots * tile * HD * 4 * 2,
            bytes_accessed=16 * tokens * width * 2,
            transcendentals=rows * slots * tile,
        ),
        name="self_attention",
    )(index, count, *k_pieces, *v_pieces, *q_pieces)


def cross_kernel(place, *refs, n_text, text_total, order):
    text = refs[:n_text]
    q_pieces = refs[n_text : n_text + 2]
    out_pieces = refs[n_text + 2 : n_text + 4]
    window, turned, scratch = refs[n_text + 4 :]
    at = 0
    for ref in text:
        rows = ref.shape[1]
        window[:, at : at + rows, :] = ref[...]
        at += rows
    start = pl.multiple_of(place[0], order)
    live = place[1]
    side = place[2]
    tokens = q_pieces[0].shape[0]
    block_rows = scratch.shape[1]
    turned[...] = jnp.transpose(window[0, pl.ds(start, text_total), :])
    column = lax.broadcasted_iota(jnp.int32, (1, text_total), 1)
    half = order // 2
    seen = jnp.where(side == 1, column ^ half, column) < live
    span = 256

    def stage(part, r):
        rows = slice(r * block_rows, (r + 1) * block_rows)

        def block(c):
            score = jnp.dot(
                q_pieces[part][rows, :], turned[:, c : c + span], preferred_element_type=F32
            )
            return jnp.where(seen[:, c : c + span], score, FAR)

        def value(c):
            return window[1, pl.ds(pl.multiple_of(start + c, order), span), :]

        def store(out):
            out_pieces[part][rows, :] = out

        return (
            [functools.partial(block, c) for c in range(0, text_total, span)],
            [functools.partial(value, c) for c in range(0, text_total, span)],
            store,
        )

    weigh([stage(part, r) for part in range(2) for r in range(tokens // block_rows)], scratch)


def cross_attention(place, text, q_pieces, text_total, order):
    tokens, width = q_pieces[0].shape
    heads = width // HD
    window_rows = sum(block.shape[1] for block in text)
    block_rows = tokens // 2
    spec = pl.BlockSpec((tokens, HD), lambda h, *_: (0, h))
    text_specs = [pl.BlockSpec((2, block.shape[1], HD), lambda h, *_: (0, 0, h)) for block in text]
    rows = 2 * tokens * heads
    return pl.pallas_call(
        functools.partial(cross_kernel, n_text=len(text), text_total=text_total, order=order),
        grid_spec=pltpu.PrefetchScalarGridSpec(
            num_scalar_prefetch=1,
            grid=(heads,),
            in_specs=text_specs + [spec] * 2,
            out_specs=[spec] * 2,
            scratch_shapes=[
                pltpu.VMEM((2, window_rows, HD), BF),
                pltpu.VMEM((HD, text_total), BF),
                pltpu.VMEM((3, block_rows, text_total), F32),
            ],
        ),
        out_shape=[jax.ShapeDtypeStruct((tokens, width), BF)] * 2,
        compiler_params=pltpu.CompilerParams(vmem_limit_bytes=VMEM),
        cost_estimate=pl.CostEstimate(
            flops=rows * text_total * HD * 4 * 2,
            bytes_accessed=4 * tokens * width * 2 + 2 * window_rows * width * 2,
            transcendentals=rows * text_total,
        ),
        name="cross_attention",
    )(place, *text, *q_pieces)


def body(
    q_raw,
    k_raw,
    v_in,
    cross_q_raw,
    text_k_raw,
    text_v,
    q_gain,
    k_gain,
    cross_q_gain,
    text_k_gain,
    nbr,
    nbr_count,
    text_len,
):
    tokens, width = q_raw.shape[1:]
    heads = width // HD
    tiles = nbr.shape[0]
    slots = nbr.shape[1]
    tile = tokens // tiles
    shards = lax.axis_size("frame")
    pairs = shards // 2
    shard = lax.axis_index("frame")
    side = shard % 2
    pair = shard // 2
    cuts = [0, (2 * heads + 4) // 5, (7 * heads + 9) // 10, heads]
    chunks = [(a * HD, b * HD) for a, b in zip(cuts, cuts[1:])]

    def partner(value):
        return lax.ppermute(value, "frame", [(i, i ^ 1) for i in range(shards)])

    def up(value, least=0):
        moves = [(i, i + 2) for i in range(shards - 2) if i // 2 >= least]
        return lax.ppermute(value, "frame", moves)

    def down(value, least=0):
        moves = [(i, i - 2) for i in range(2, shards) if i // 2 < pairs - least]
        return lax.ppermute(value, "frame", moves)

    def mine(value):
        return lax.dynamic_index_in_dim(value, side, 0, keepdims=False)

    def theirs(value):
        return lax.dynamic_index_in_dim(value, 1 - side, 0, keepdims=False)

    def after(value, *others):
        return lax.optimization_barrier((value, *others))[0]

    meta = jnp.concatenate([nbr, nbr_count[:, None]], axis=1)
    got_meta = partner(meta)
    meta = jnp.concatenate([meta, got_meta], axis=0)
    neighbour, count = meta[:, :slots], meta[:, slots]
    near_shard = neighbour // tiles
    index = (
        (near_shard // 2 - pair + 1) * (2 * tiles)
        + ((near_shard % 2) ^ side) * tiles
        + neighbour % tiles
    )
    index = jnp.clip(index, 0, 6 * tiles - 1).reshape(-1)
    v_keep, v_send = mine(v_in), theirs(v_in)
    v_got = partner(v_send)
    v_up, v_down = up(v_keep), down(v_keep)

    q_late, k_late, cq_late, text_late = (
        after(t, v_keep, v_send) for t in (q_raw, k_raw, cross_q_raw, text_k_raw)
    )
    sums = jnp.concatenate([squares(t) for t in (q_late, k_late, cq_late, text_late)], axis=1)
    totals = lax.psum(sums, "head")
    v_got_up, v_got_down = up(v_got), down(v_got)
    v_pieces = [v_up, v_got_up, v_keep, v_got, v_down, v_got_down]

    text_factor = lax.rsqrt(totals[:, 3 * tokens :] / D + EPSILON)[:, :, None]
    text_keys = (text_k_raw.astype(F32) * text_factor * text_k_gain).astype(BF)
    shard_text = text_keys.shape[1]
    text_total = shard_text * shards
    text_both = jnp.stack([text_keys, text_v], axis=1)
    order = 2 * shard_text
    relayed = pairs <= 4
    if relayed:
        text_got = partner(after(theirs(text_both), v_got))
        text_pair = jnp.concatenate([mine(text_both), text_got], axis=1)
        start, text_side = (pairs - 1 - pair) * order, side
    else:
        gathered = lax.all_gather(text_both, "frame", axis=2, tiled=True)
        text_got = mine(gathered)
        start, text_side = jnp.zeros_like(pair), jnp.zeros_like(side)
    place = jnp.stack([start, text_len[side], text_side]).astype(jnp.int32)

    keep_q, keep_k, keep_cq, send_q, send_k, send_cq = pack(
        jnp.reshape(side, (1,)),
        after(totals[:, : 3 * tokens].reshape(2, 3, 1, tokens), v_got, got_meta),
        jnp.stack([q_gain, k_gain, cross_q_gain]),
        (q_raw, k_raw, cross_q_raw),
    )
    got_cq = partner(after(send_cq, v_up, v_down))
    got_k = partner(after(send_k, text_got, v_got_up, v_got_down))
    got_q = partner(after(send_q, got_cq))
    cross_pieces = [keep_cq, got_cq]
    q_pieces = [keep_q, got_q]

    if relayed:
        text_pair = after(text_pair, v_up, v_down)
        ups, downs = [text_pair], [text_pair]
        for step in range(pairs - 1):
            ups.append(up(ups[-1], step))
            downs.append(down(downs[-1], step))
        text = ups[:0:-1] + [text_pair] + downs[1:]
    else:
        text = [text_got]
    joined_k = join(keep_k, got_k, chunks)
    k_pieces = []
    for number, own in enumerate(joined_k):
        if number < 2:
            own = after(own, *text[max(0, 1 - number) : len(text) - max(0, 1 - number)])
        else:
            own = after(own, *k_pieces[number - 2])
        k_pieces.append([up(own), own, down(own)])

    cross_keep, cross_send = cross_attention(place, text, cross_pieces, text_total, order)
    cross_got = partner(after(cross_send, got_q))
    self_keep, self_got = [], []
    for number, chunk in enumerate(chunks):
        out_keep, out_send = self_attention(
            index,
            count,
            [after(k, cross_keep, *self_keep) for k in k_pieces[number]],
            v_pieces,
            q_pieces,
            chunk[0] // HD,
            tile,
            slots,
        )
        self_keep.append(out_keep)
        self_got.append(partner(out_send))

    def joined(own, got):
        rows = jnp.arange(2, dtype=jnp.int32)[:, None, None] == side
        return jnp.where(rows, own[None], got[None])

    self_out = jnp.concatenate([joined(a, b) for a, b in zip(self_keep, self_got)], axis=2)
    return (self_out, joined(cross_keep, cross_got))


def solution(mesh):
    in_specs = (
        P(None, "frame", "head"),
        P(None, "frame", "head"),
        P(None, "frame", "head"),
        P(None, "frame", "head"),
        P(None, "frame", "head"),
        P(None, "frame", "head"),
        P("head"),
        P("head"),
        P("head"),
        P("head"),
        P("frame", None),
        P("frame"),
        P(),
    )
    out_specs = (P(None, "frame", "head"), P(None, "frame", "head"))
    return jax.shard_map(body, mesh=mesh, in_specs=in_specs, out_specs=out_specs, check_vma=False)
```

time: 807 us -> 195 us (0.24)
  local copies, waits for them, and re-layouts: 311 us -> 8.95 us
  waiting for transfers between devices: 267 us -> 50.7 us
  matrix products: 101 us -> 0 us
  Pallas kernels: 0 us -> 59.5 us
  other arithmetic: 62 us -> 7.08 us
  starting transfers between devices: 24 us -> 54.2 us
  between operations: 14.2 us -> 1.16 us
  loops' own time: 8.14 us -> 0 us
    ppermute x8 -> x26, waiting for transfers between devices: 267 us -> 50.7 us  [the longest x10 29.1 us: partner(): return lax.ppermute(value, 'frame', [(i, i ^ 1) for i in range(shards)])]
    reshape x6 -> x2, local copies, waits for them, and re-layouts: 97.5 us -> 1.21 us  [the longest x1 0.61 us: body(): totals[:, :3 * tokens].reshape(2, 3, 1, tokens)]
    select_n x6 -> x0, local copies, waits for them, and re-layouts: 95.5 us -> none  [the longest x3 47.9 us: one_tile(): jnp.take(value_tiles, slot_list, axis=1)]
    pallas_call x0 -> x6, Pallas kernels: none -> 59.5 us  [the longest x3 35.1 us: self_attention(): pl.pallas_call(functools.partial(self_kernel, tile=tile, slots=slots, n_k...]
    gather x6 -> x0, local copies, waits for them, and re-layouts: 54.3 us -> none  [the longest x3 27.3 us: one_tile(): jnp.take(key_tiles, slot_list, axis=1).reshape(2, NB * tile_len, groups, HD)]
    sub x6 -> x0, matrix products: 54.3 us -> none  [soft_weights(): powers = jnp.exp(scores - row_top)]
    dot_general x6 -> x0, matrix products: 47.1 us -> none  [the longest x3 34.3 us: one_tile(): jnp.einsum('chqk,ckhd->cqhd', self_weights, chosen_values, preferred_elem...]
    select_n x3, other arithmetic: 44.7 us -> 1.89 us  [joined(): return jnp.where(rows, own[None], got[None])]
  transfers between devices with their start and end apart: 10 -> 26, of which waited for: 4 -> 11; matrix products, arithmetic and copies ran while one was open for 5% -> 4% of each run, Pallas kernels for 0% -> 31%
where the time goes in v1:
time: 195 us; the launch traced here: 193 us
  Pallas kernels  59.5 us (31%)
  starting transfers between devices  54.2 us (28%)
  waiting for transfers between devices  50.7 us (26%)
  blocking collectives  11.1 us (6%)
  local copies, waits for them, and re-layouts  8.95 us (5%)
  other arithmetic  7.08 us (4%)
    pallas_call x3, Pallas kernels, self_attention(): pl.pallas_call(functools.partial(self_kernel, tile=tile, slots=slots, n_k...  35.1 us
    ppermute x8, starting transfers between devices, up(): return lax.ppermute(value, 'frame', moves)  32.6 us
    ppermute x10, waiting for transfers between devices, partner(): return lax.ppermute(value, 'frame', [(i, i ^ 1) for i in range(shards)])  29.1 us
    ppermute x8, waiting for transfers between devices, down(): return lax.ppermute(value, 'frame', moves)  15.4 us
    pallas_call x1, Pallas kernels, cross_attention(): pl.pallas_call(functools.partial(cross_kernel, n_text=len(text), text_tot...  14 us
    ppermute x10, starting transfers between devices, partner(): return lax.ppermute(value, 'frame', [(i, i ^ 1) for i in range(shards)])  11.2 us
    psum x1, blocking collectives, body(): totals = lax.psum(sums, 'head')  11.1 us
    ppermute x8, starting transfers between devices, down(): return lax.ppermute(value, 'frame', moves)  10.5 us
  transfers between devices with their start and end apart: 26, of which 11 were waited for; matrix products, arithmetic and copies ran while one was open for 4% of the time, Pallas kernels for 31%

profile of v1, /device:TPU:0, one launch (start us, length us, event | category | flops | bytes accessed | tf_op | source)
XLA Modules:
  0.0 192.7 jit_solution(12209305025224796833)
XLA Ops:
  0.7 2.7 %dynamic-slice_bitcast_fusion = (bf16[384,1280]{1,0:T(8,128)(2,1)}, bf16[384,1280]{1,0:T(8,128)(2,1)S(1)}) fusion(bf16[2,384,1280]{2,1,0:T(8,128)(2,1)} %param.15, s32[]{:T(128)S(6)} %select_n.62, s32[]{:T(128)S(6)} %select_n.61), kind=kLoop, calls=%fused_computation.5 | loop fusion | bytes 3932168 | tf_op jit(solution)/shard_map/jit(dynamic_index_in_dim)/squeeze | solution.py:351
  3.4 5.2 %collective-permute-start.6 = (bf16[384,1280]{1,0:T(8,128)(2,1)S(1)}, bf16[384,1280]{1,0:T(8,128)(2,1)S(1)}, u32[]{:S(2)}, u32[]{:S(2)}) collective-permute-start(bf16[384,1280]{1,0:T(8,128)(2,1)S(1)} %get-tuple-element.83.refs_5_), channel_id=1, source_target_pairs={{0,8},{4,12},{8,16},{12,20},{16,24},{20,28},{1,9},{5,13},{9,17},{1... | collective-permute-start | bytes 2949128 | tf_op jit(solution)/shard_map/ppermute | solution.py:341
  8.7 1.3 collective-permute-start.7
  10.0 1.6 collective-permute-start.1
  12.2 0.8 multiply_reduce_fusion
  13.1 11.1 %psum.7 = f32[2,1216]{1,0:T(2,128)S(1)} all-reduce(f32[2,1216]{1,0:T(2,128)S(1)} %pad_maximum_fusion.3), channel_id=1, replica_groups=mesh['frame'=8,'head'=4] {'head'}, use_global_device_ids=true, to_apply=%region_4.5 | all-reduce | flops 2432 | bytes 19456 | tf_op jit(solution)/shard_map/psum | solution.py:375
  24.5 9.1 %collective-permute-done.1.refs_6_ = bf16[384,1280]{1,0:T(8,128)(2,1)} collective-permute-done((bf16[384,1280]{1,0:T(8,128)(2,1)}, bf16[384,1280]{1,0:T(8,128)(2,1)}, u32[]{:S(2)}, u32[]{:S(2)}) %collective-permute-start.1) | collective-permute-done | bytes 983072 | tf_op jit(solution)/shard_map/ppermute | solution.py:337
  33.6 1.5 collective-permute-start.2
  35.1 5.2 %collective-permute-start.3 = (bf16[384,1280]{1,0:T(8,128)(2,1)}, bf16[384,1280]{1,0:T(8,128)(2,1)}, u32[]{:S(2)}, u32[]{:S(2)}) collective-permute-start(bf16[384,1280]{1,0:T(8,128)(2,1)} %collective-permute-done.1.refs_6_), channel_id=1, source_target_pairs={{0,8},{4,12},{8,16},{12,20},{16,24},{20,28},{1,9},{5,13},{9,17},{1... | collective-permute-start | bytes 2949128 | tf_op jit(solution)/shard_map/ppermute | solution.py:341
  40.3 1.3 collective-permute-start.4
  41.9 5.3 %collective-permute-start.8 = (bf16[2,128,1280]{2,1,0:T(8,128)(2,1)S(1)}, bf16[2,128,1280]{2,1,0:T(8,128)(2,1)}, u32[]{:S(2)}, u32[]{:S(2)}) collective-permute-start(bf16[2,128,1280]{2,1,0:T(8,128)(2,1)S(1)} %pad_maximum_fusion.1.refs_3_), channel_id=1, source_target_pairs={{0,8},{4,12},{8,16},{12,20},{16,24},{20,28},{1,9},{5,13},{9,17},{1... | collective-permute-start | bytes 1966088 | tf_op jit(solution)/shard_map/ppermute | solution.py:341
  47.2 1.3 collective-permute-start.10
  48.6 1.1 collective-permute-start
  50.9 1.2 collective-permute-done
  52.2 7.5 %norm_pack.1 = (bf16[384,1280]{1,0:T(8,128)(2,1)}, bf16[384,1280]{1,0:T(8,128)(2,1)}, bf16[384,1280]{1,0:T(8,128)(2,1)}, bf16[384,1280]{1,0:T(8,128)(2,1)}, bf16...) custom-call(s32[1]{0:T(128)} %bitcast.1.side, f32[2,3,1,384]{3,2,1,0:T(1,128)} %reshape.30.totals, ...), custom_call_target="tpu_custom_call" | custom-call | bytes 11796480 | tf_op jit(solution)/shard_map/norm_pack/pallas_call | solution.py:103
  59.7 1.1 collective-permute-start.15
  60.8 1.0 collective-permute-done.3.refs_4_
  61.9 5.3 %collective-permute-done.4.refs_8_ = bf16[384,1280]{1,0:T(8,128)(2,1)} collective-permute-done((bf16[384,1280]{1,0:T(8,128)(2,1)}, bf16[384,1280]{1,0:T(8,128)(2,1)}, u32[]{:S(2)}, u32[]{:S(2)}) %collective-permute-start.4) | collective-permute-done | bytes 983072 | tf_op jit(solution)/shard_map/ppermute | solution.py:345
  67.7 5.1 %collective-permute-done.8.refs_2_ = bf16[2,128,1280]{2,1,0:T(8,128)(2,1)} collective-permute-done((bf16[2,128,1280]{2,1,0:T(8,128)(2,1)S(1)}, bf16[2,128,1280]{2,1,0:T(8,128)(2,1)}, u32[]{:S(2)}, u32[]{:S(2)}) %collective-permute-start.8) | collective-permute-done | bytes 655392 | tf_op jit(solution)/shard_map/ppermute | solution.py:341
  72.8 1.5 collective-permute-start.9
  74.4 3.6 %collective-permute-done.10.refs_4_ = bf16[2,128,1280]{2,1,0:T(8,128)(2,1)} collective-permute-done((bf16[2,128,1280]{2,1,0:T(8,128)(2,1)S(1)}, bf16[2,128,1280]{2,1,0:T(8,128)(2,1)}, u32[]{:S(2)}, u32[]{:S(2)}) %collective-permute-start.10) | collective-permute-done | bytes 655392 | tf_op jit(solution)/shard_map/ppermute | solution.py:345
  78.0 1.3 collective-permute-start.11
  79.3 5.4 %collective-permute-done.15.refs_8_ = bf16[384,1280]{1,0:T(8,128)(2,1)S(1)} collective-permute-done((bf16[384,1280]{1,0:T(8,128)(2,1)}, bf16[384,1280]{1,0:T(8,128)(2,1)S(1)}, u32[]{:S(2)}, u32[]{:S(2)}) %collective-permute-start.15) | collective-permute-done | bytes 983072 | tf_op jit(solution)/shard_map/ppermute | solution.py:337
  84.7 1.1 collective-permute-start.17
  85.7 1.5 collective-permute-start.13
  87.3 6.4 %collective-permute-done.11.refs_5_ = bf16[2,128,1280]{2,1,0:T(8,128)(2,1)} collective-permute-done((bf16[2,128,1280]{2,1,0:T(8,128)(2,1)}, bf16[2,128,1280]{2,1,0:T(8,128)(2,1)}, u32[]{:S(2)}, u32[]{:S(2)}) %collective-permute-start.11) | collective-permute-done | bytes 655392 | tf_op jit(solution)/shard_map/ppermute | solution.py:345
  93.7 1.3 collective-permute-start.14
  95.6 1.2 pad_add_fusion.2.place
  96.9 8.9 %collective-permute-done.5.second = bf16[384,1280]{1,0:T(8,128)(2,1)S(1)} collective-permute-done((bf16[384,1280]{1,0:T(8,128)(2,1)}, bf16[384,1280]{1,0:T(8,128)(2,1)S(1)}, u32[]{:S(2)}, u32[]{:S(2)}) %collective-permute-start.5) | collective-permute-done | bytes 983072 | tf_op jit(solution)/shard_map/ppermute | solution.py:337
  105.7 1.0 copy-done.5
  106.7 2.9 %join.1 = (bf16[768,512]{1,0:T(8,128)(2,1)}, bf16[768,384]{1,0:T(8,128)(2,1)}, bf16[768,384]{1,0:T(8,128)(2,1)}) custom-call(bf16[384,1280]{1,0:T(8,128)(2,1)} %get-tuple-element.47.first, bf16[384,1280]{1,0:T(8,128)(2,1)} %copy-done.5), custom_call_target="tpu_custom_call" | custom-call | bytes 3932160 | tf_op jit(solution)/shard_map/join/pallas_call | solution.py:131
  109.6 4.6 %collective-permute-start.12 = (bf16[768,512]{1,0:T(8,128)(2,1)}, bf16[768,512]{1,0:T(8,128)(2,1)S(1)}, u32[]{:S(2)}, u32[]{:S(2)}) collective-permute-start(bf16[768,512]{1,0:T(8,128)(2,1)} %get-tuple-element.59.refs_1_), channel_id=1, source_target_pairs={{0,8},{4,12},{8,16},{12,20},{16,24},{20,28},{1,9},{5,13},{9,17},{1... | collective-permute-start | bytes 2359304 | tf_op jit(solution)/shard_map/ppermute | solution.py:341
  114.2 1.3 collective-permute-start.16
  116.9 4.6 %collective-permute-start.19 = (bf16[768,384]{1,0:T(8,128)(2,1)}, bf16[768,384]{1,0:T(8,128)(2,1)S(1)}, u32[]{:S(2)}, u32[]{:S(2)}) collective-permute-start(bf16[768,384]{1,0:T(8,128)(2,1)} %get-tuple-element.69.refs_1_), channel_id=1, source_target_pairs={{0,8},{4,12},{8,16},{12,20},{16,24},{20,28},{1,9},{5,13},{9,17},{1... | collective-permute-start | bytes 1769480 | tf_op jit(solution)/shard_map/ppermute | solution.py:341
  121.5 1.3 collective-permute-start.20
  122.8 14.0 %cross_attention.1 = (bf16[384,1280]{1,0:T(8,128)(2,1)}, bf16[384,1280]{1,0:T(8,128)(2,1)}) custom-call(s32[3]{0:T(128)} %pad_add_fusion.2.place, bf16[2,128,1280]{2,1,0:T(8,128)(2,1)} %collective-permute-done.13.refs_0_, bf16[2,128,1280]{2,1,0:T(8,128)(2,1)} %collective-permute-done.9.refs_1_, bf16[2,128,1280]{2,1,0:T(8,128)(2,1)} %collective-permute-done.8.refs_2_, ...), custom_call_target="tpu_custom_call" | custom-call | flops 4026531840 | bytes 8519680 | tf_op jit(solution)/shard_map/cross_attention/pallas_call | solution.py:284
  136.8 1.1 collective-permute-start.25
  138.0 4.6 %collective-permute-start.22 = (bf16[768,384]{1,0:T(8,128)(2,1)S(1)}, bf16[768,384]{1,0:T(8,128)(2,1)S(1)}, u32[]{:S(2)}, u32[]{:S(2)}) collective-permute-start(bf16[768,384]{1,0:T(8,128)(2,1)S(1)} %copy-done.22), channel_id=1, source_target_pairs={{0,8},{4,12},{8,16},{12,20},{16,24},{20,28},{1,9},{5,13},{9,17},{1... | collective-permute-start | bytes 1769480 | tf_op jit(solution)/shard_map/ppermute | solution.py:341
  142.6 1.5 collective-permute-start.23
  144.1 13.5 %self_attention.3 = (bf16[384,512]{1,0:T(8,128)(2,1)}, bf16[384,512]{1,0:T(8,128)(2,1)}) custom-call(s32[84]{0:T(128)} %reshape.28.index, s32[6]{0:T(128)} %slice_reduce_fusion.count, bf16[768,512]{1,0:T(8,128)(2,1)} %copy-done.21, bf16[768,512]{1,0:T(8,128)(2,1)} %get-tuple-element.59.refs_1_, bf16[768,512]{1,0:T(8,128)(2,1)} %collective-permute-done.16.refs_2_, ...), custom_call_target="tpu_custom_call" | custom-call | flops 5637144576 | bytes 6291456 | tf_op jit(solution)/shard_map/self_attention/pallas_call | solution.py:204
  157.6 1.0 collective-permute-start.18
  159.4 10.8 %self_attention.4 = (bf16[384,384]{1,0:T(8,128)(2,1)}, bf16[384,384]{1,0:T(8,128)(2,1)}) custom-call(s32[84]{0:T(128)} %reshape.28.index, s32[6]{0:T(128)} %slice_reduce_fusion.count, bf16[768,384]{1,0:T(8,128)(2,1)} %copy-done.23, bf16[768,384]{1,0:T(8,128)(2,1)} %get-tuple-element.69.refs_1_, bf16[768,384]{1,0:T(8,128)(2,1)} %copy-done.24, ...), custom_call_target="tpu_custom_call" | custom-call | flops 4227858432 | bytes 4718592 | tf_op jit(solution)/shard_map/self_attention/pallas_call | solution.py:204
  170.2 1.1 collective-permute-start.21
  173.2 10.8 %self_attention.5 = (bf16[384,384]{1,0:T(8,128)(2,1)}, bf16[384,384]{1,0:T(8,128)(2,1)}) custom-call(s32[84]{0:T(128)} %reshape.28.index, s32[6]{0:T(128)} %slice_reduce_fusion.count, bf16[768,384]{1,0:T(8,128)(2,1)} %copy-done.25, bf16[768,384]{1,0:T(8,128)(2,1)} %get-tuple-element.76.refs_1_, bf16[768,384]{1,0:T(8,128)(2,1)} %copy-done.26, ...), custom_call_target="tpu_custom_call" | custom-call | flops 4227858432 | bytes 4718592 | tf_op jit(solution)/shard_map/self_attention/pallas_call | solution.py:204
  184.0 1.0 collective-permute-start.24
  185.1 1.5 broadcast_select_fusion
  186.6 4.4 %collective-permute-done.24 = bf16[384,384]{1,0:T(8,128)(2,1)S(1)} collective-permute-done((bf16[384,384]{1,0:T(8,128)(2,1)}, bf16[384,384]{1,0:T(8,128)(2,1)S(1)}, u32[]{:S(2)}, u32[]{:S(2)}) %collective-permute-start.24) | collective-permute-done | bytes 294944 | tf_op jit(solution)/shard_map/ppermute | solution.py:337
  191.3 1.4 pad_maximum_fusion
  (95 shorter events, 8.0 us)
Async XLA Ops:
  0.6 10.9 %copy-start.3 = (bf16[2,64,1280]{2,1,0:T(8,128)(2,1)S(1)}, bf16[2,64,1280]{2,1,0:T(8,128)(2,1)}, u32[]{:S(2)}) copy-start(bf16[2,64,1280]{2,1,0:T(8,128)(2,1)} %param.17) | copy-start | bytes 983044
  0.7 11.0 %copy-start.2 = (bf16[2,384,1280]{2,1,0:T(8,128)(2,1)S(1)}, bf16[2,384,1280]{2,1,0:T(8,128)(2,1)}, u32[]{:S(2)}) copy-start(bf16[2,384,1280]{2,1,0:T(8,128)(2,1)} %refs_0_.1) | copy-start | bytes 5898244
  0.7 11.5 %copy-start.1 = (bf16[2,384,1280]{2,1,0:T(8,128)(2,1)S(1)}, bf16[2,384,1280]{2,1,0:T(8,128)(2,1)}, u32[]{:S(2)}) copy-start(bf16[2,384,1280]{2,1,0:T(8,128)(2,1)} %refs_1_.1) | copy-start | bytes 5898244
  3.4 9.6 %copy-start.4 = (bf16[384,1280]{1,0:T(8,128)(2,1)}, bf16[384,1280]{1,0:T(8,128)(2,1)S(1)}, u32[]{:S(2)}) copy-start(bf16[384,1280]{1,0:T(8,128)(2,1)S(1)} %get-tuple-element.83.refs_5_) | copy-start | bytes 2949124
  3.4 8.8 %copy-start = (bf16[2,384,1280]{2,1,0:T(8,128)(2,1)S(1)}, bf16[2,384,1280]{2,1,0:T(8,128)(2,1)}, u32[]{:S(2)}) copy-start(bf16[2,384,1280]{2,1,0:T(8,128)(2,1)} %refs_2_.1) | copy-start | bytes 5898244
  3.4 38.5 %collective-permute-start.6 = (bf16[384,1280]{1,0:T(8,128)(2,1)S(1)}, bf16[384,1280]{1,0:T(8,128)(2,1)S(1)}, u32[]{:S(2)}, u32[]{:S(2)}) collective-permute-start(bf16[384,1280]{1,0:T(8,128)(2,1)S(1)} %get-tuple-element.83.refs_5_), channel_id=1, source_target_pairs={{0,8},{4,12},{8,16},{12,20},{16,24},{20,28},{1,9},{5,13},{9,17},{1... | collective-permute-start | bytes 2949128 | tf_op jit(solution)/shard_map/ppermute | solution.py:341
  8.7 33.2 %collective-permute-start.7 = (bf16[384,1280]{1,0:T(8,128)(2,1)S(1)}, bf16[384,1280]{1,0:T(8,128)(2,1)}, u32[]{:S(2)}, u32[]{:S(2)}) collective-permute-start(bf16[384,1280]{1,0:T(8,128)(2,1)S(1)} %get-tuple-element.83.refs_5_), channel_id=1, source_target_pairs={{8,0},{12,4},{16,8},{20,12},{24,16},{28,20},{9,1},{13,5},{17,9},{2... | collective-permute-start | bytes 2949128 | tf_op jit(solution)/shard_map/ppermute | solution.py:345
  10.0 23.6 %collective-permute-start.1 = (bf16[384,1280]{1,0:T(8,128)(2,1)}, bf16[384,1280]{1,0:T(8,128)(2,1)}, u32[]{:S(2)}, u32[]{:S(2)}) collective-permute-start(bf16[384,1280]{1,0:T(8,128)(2,1)} %get-tuple-element.82), channel_id=1, source_target_pairs={{0,4},{4,0},{8,12},{12,8},{16,20},{20,16},{24,28},{28,24},{1,5},{5... | collective-permute-start | bytes 2949128 | tf_op jit(solution)/shard_map/ppermute | solution.py:337
  12.2 12.1 %copy-start.16 = (f32[1280]{0:T(1024)S(1)}, f32[1280]{0:T(1024)}, u32[]{:S(2)}) copy-start(f32[1280]{0:T(1024)} %param.22) | copy-start | bytes 15364
  12.2 12.2 %copy-start.9 = (bf16[2,64,1280]{2,1,0:T(8,128)(2,1)S(1)}, bf16[2,64,1280]{2,1,0:T(8,128)(2,1)}, u32[]{:S(2)}) copy-start(bf16[2,64,1280]{2,1,0:T(8,128)(2,1)} %param.18) | copy-start | bytes 983044
  13.1 28.5 %copy-start.17 = (s32[3]{0:T(128)S(1)}, s32[3]{0:T(128)}, u32[]{:S(2)}) copy-start(s32[3]{0:T(128)} %param.24) | copy-start | bytes 40
  13.1 35.4 %copy-start.12 = (s32[3,14]{1,0:T(4,128)S(1)}, s32[3,14]{1,0:T(4,128)}, u32[]{:S(2)}) copy-start(s32[3,14]{1,0:T(4,128)} %param.23) | copy-start | bytes 508
  13.1 36.6 %copy-start.13 = (f32[1280]{0:T(1024)S(1)}, f32[1280]{0:T(1024)}, u32[]{:S(2)}) copy-start(f32[1280]{0:T(1024)} %param.21) | copy-start | bytes 15364
  13.1 36.6 %copy-start.14 = (f32[1280]{0:T(1024)S(1)}, f32[1280]{0:T(1024)}, u32[]{:S(2)}) copy-start(f32[1280]{0:T(1024)} %param.20) | copy-start | bytes 15364
  13.1 36.6 %copy-start.15 = (f32[1280]{0:T(1024)S(1)}, f32[1280]{0:T(1024)}, u32[]{:S(2)}) copy-start(f32[1280]{0:T(1024)} %param.19) | copy-start | bytes 15364
  33.6 8.3 %collective-permute-start.2 = (bf16[2,64,1280]{2,1,0:T(8,128)(2,1)S(1)}, bf16[2,64,1280]{2,1,0:T(8,128)(2,1)S(1)}, u32[]{:S(2)}, u32[]{:S(2)}) collective-permute-start(bf16[2,64,1280]{2,1,0:T(8,128)(2,1)S(1)} %get-tuple-element.49), channel_id=1, source_target_pairs={{0,4},{4,0},{8,12},{12,8},{16,20},{20,16},{24,28},{28,24},{1,5},{5... | collective-permute-start | bytes 983048 | tf_op jit(solution)/shard_map/ppermute | solution.py:337
  35.1 26.8 %collective-permute-start.3 = (bf16[384,1280]{1,0:T(8,128)(2,1)}, bf16[384,1280]{1,0:T(8,128)(2,1)}, u32[]{:S(2)}, u32[]{:S(2)}) collective-permute-start(bf16[384,1280]{1,0:T(8,128)(2,1)} %collective-permute-done.1.refs_6_), channel_id=1, source_target_pairs={{0,8},{4,12},{8,16},{12,20},{16,24},{20,28},{1,9},{5,13},{9,17},{1... | collective-permute-start | bytes 2949128 | tf_op jit(solution)/shard_map/ppermute | solution.py:341
  40.3 26.9 %collective-permute-start.4 = (bf16[384,1280]{1,0:T(8,128)(2,1)}, bf16[384,1280]{1,0:T(8,128)(2,1)}, u32[]{:S(2)}, u32[]{:S(2)}) collective-permute-start(bf16[384,1280]{1,0:T(8,128)(2,1)} %collective-permute-done.1.refs_6_), channel_id=1, source_target_pairs={{8,0},{12,4},{16,8},{20,12},{24,16},{28,20},{9,1},{13,5},{17,9},{2... | collective-permute-start | bytes 2949128 | tf_op jit(solution)/shard_map/ppermute | solution.py:345
  41.9 17.8 %copy-start.7 = (bf16[2,128,1280]{2,1,0:T(8,128)(2,1)}, bf16[2,128,1280]{2,1,0:T(8,128)(2,1)S(1)}, u32[]{:S(2)}) copy-start(bf16[2,128,1280]{2,1,0:T(8,128)(2,1)S(1)} %pad_maximum_fusion.1.refs_3_) | copy-start | bytes 1966084
  41.9 17.8 %copy-start.18 = (bf16[384,1280]{1,0:T(8,128)(2,1)}, bf16[384,1280]{1,0:T(8,128)(2,1)S(1)}, u32[]{:S(2)}) copy-start(bf16[384,1280]{1,0:T(8,128)(2,1)S(1)} %collective-permute-done.6.refs_3_) | copy-start | bytes 2949124
  41.9 30.9 %collective-permute-start.8 = (bf16[2,128,1280]{2,1,0:T(8,128)(2,1)S(1)}, bf16[2,128,1280]{2,1,0:T(8,128)(2,1)}, u32[]{:S(2)}, u32[]{:S(2)}) collective-permute-start(bf16[2,128,1280]{2,1,0:T(8,128)(2,1)S(1)} %pad_maximum_fusion.1.refs_3_), channel_id=1, source_target_pairs={{0,8},{4,12},{8,16},{12,20},{16,24},{20,28},{1,9},{5,13},{9,17},{1... | collective-permute-start | bytes 1966088 | tf_op jit(solution)/shard_map/ppermute | solution.py:341
  47.2 30.8 %collective-permute-start.10 = (bf16[2,128,1280]{2,1,0:T(8,128)(2,1)S(1)}, bf16[2,128,1280]{2,1,0:T(8,128)(2,1)}, u32[]{:S(2)}, u32[]{:S(2)}) collective-permute-start(bf16[2,128,1280]{2,1,0:T(8,128)(2,1)S(1)} %pad_maximum_fusion.1.refs_3_), channel_id=1, source_target_pairs={{8,0},{12,4},{16,8},{20,12},{24,16},{28,20},{9,1},{13,5},{17,9},{2... | collective-permute-start | bytes 1966088 | tf_op jit(solution)/shard_map/ppermute | solution.py:345
  48.6 3.6 %collective-permute-start = (s32[3,15]{1,0:T(4,128)S(1)}, s32[3,15]{1,0:T(4,128)S(1)}, u32[]{:S(2)}, u32[]{:S(2)}) collective-permute-start(s32[3,15]{1,0:T(4,128)S(1)} %pad_add_fusion.1), channel_id=1, source_target_pairs={{0,4},{4,0},{8,12},{12,8},{16,20},{20,16},{24,28},{28,24},{1,5},{5... | collective-permute-start | bytes 548 | tf_op jit(solution)/shard_map/ppermute | solution.py:337
  52.2 42.8 %copy-start.27 = (s32[2]{0:T(128)S(1)}, s32[2]{0:T(128)}, u32[]{:S(2)}) copy-start(s32[2]{0:T(128)} %param.25) | copy-start | bytes 28
  59.7 25.0 %collective-permute-start.15 = (bf16[384,1280]{1,0:T(8,128)(2,1)}, bf16[384,1280]{1,0:T(8,128)(2,1)S(1)}, u32[]{:S(2)}, u32[]{:S(2)}) collective-permute-start(bf16[384,1280]{1,0:T(8,128)(2,1)} %get-tuple-element.56), channel_id=1, source_target_pairs={{0,4},{4,0},{8,12},{12,8},{16,20},{20,16},{24,28},{28,24},{1,5},{5... | collective-permute-start | bytes 2949128 | tf_op jit(solution)/shard_map/ppermute | solution.py:337
  67.2 38.5 %collective-permute-start.5 = (bf16[384,1280]{1,0:T(8,128)(2,1)}, bf16[384,1280]{1,0:T(8,128)(2,1)S(1)}, u32[]{:S(2)}, u32[]{:S(2)}) collective-permute-start(bf16[384,1280]{1,0:T(8,128)(2,1)} %get-tuple-element.50), channel_id=1, source_target_pairs={{0,4},{4,0},{8,12},{12,8},{16,20},{20,16},{24,28},{28,24},{1,5},{5... | collective-permute-start | bytes 2949128 | tf_op jit(solution)/shard_map/ppermute | solution.py:337
  72.8 12.9 %collective-permute-start.9 = (bf16[2,128,1280]{2,1,0:T(8,128)(2,1)}, bf16[2,128,1280]{2,1,0:T(8,128)(2,1)}, u32[]{:S(2)}, u32[]{:S(2)}) collective-permute-start(bf16[2,128,1280]{2,1,0:T(8,128)(2,1)} %collective-permute-done.8.refs_2_), channel_id=1, source_target_pairs={{8,16},{12,20},{16,24},{20,28},{9,17},{13,21},{17,25},{21,29},{10,... | collective-permute-start | bytes 1966088 | tf_op jit(solution)/shard_map/ppermute | solution.py:341
  78.0 15.7 %collective-permute-start.11 = (bf16[2,128,1280]{2,1,0:T(8,128)(2,1)}, bf16[2,128,1280]{2,1,0:T(8,128)(2,1)}, u32[]{:S(2)}, u32[]{:S(2)}) collective-permute-start(bf16[2,128,1280]{2,1,0:T(8,128)(2,1)} %collective-permute-done.10.refs_4_), channel_id=1, source_target_pairs={{8,0},{12,4},{16,8},{20,12},{9,1},{13,5},{17,9},{21,13},{10,2},{14... | collective-permute-start | bytes 1966088 | tf_op jit(solution)/shard_map/ppermute | solution.py:345
  84.7 38.1 %copy-start.20 = (bf16[384,1280]{1,0:T(8,128)(2,1)}, bf16[384,1280]{1,0:T(8,128)(2,1)S(1)}, u32[]{:S(2)}) copy-start(bf16[384,1280]{1,0:T(8,128)(2,1)S(1)} %collective-permute-done.15.refs_8_) | copy-start | bytes 2949124
  84.7 52.1 %collective-permute-start.17 = (bf16[384,1280]{1,0:T(8,128)(2,1)}, bf16[384,1280]{1,0:T(8,128)(2,1)S(1)}, u32[]{:S(2)}, u32[]{:S(2)}) collective-permute-start(bf16[384,1280]{1,0:T(8,128)(2,1)} %get-tuple-element.63), channel_id=1, source_target_pairs={{0,4},{4,0},{8,12},{12,8},{16,20},{20,16},{24,28},{28,24},{1,5},{5... | collective-permute-start | bytes 2949128 | tf_op jit(solution)/shard_map/ppermute | solution.py:337
  85.7 31.2 %collective-permute-start.13 = (bf16[2,128,1280]{2,1,0:T(8,128)(2,1)}, bf16[2,128,1280]{2,1,0:T(8,128)(2,1)}, u32[]{:S(2)}, u32[]{:S(2)}) collective-permute-start(bf16[2,128,1280]{2,1,0:T(8,128)(2,1)} %collective-permute-done.9.refs_1_), channel_id=1, source_target_pairs={{16,24},{20,28},{17,25},{21,29},{18,26},{22,30},{19,27},{23,31}} | collective-permute-start | bytes 1966088 | tf_op jit(solution)/shard_map/ppermute | solution.py:341
  93.7 23.2 %collective-permute-start.14 = (bf16[2,128,1280]{2,1,0:T(8,128)(2,1)}, bf16[2,128,1280]{2,1,0:T(8,128)(2,1)}, u32[]{:S(2)}, u32[]{:S(2)}) collective-permute-start(bf16[2,128,1280]{2,1,0:T(8,128)(2,1)} %collective-permute-done.11.refs_5_), channel_id=1, source_target_pairs={{8,0},{12,4},{9,1},{13,5},{10,2},{14,6},{11,3},{15,7}} | collective-permute-start | bytes 1966088 | tf_op jit(solution)/shard_map/ppermute | solution.py:345
  109.6 28.4 %collective-permute-start.12 = (bf16[768,512]{1,0:T(8,128)(2,1)}, bf16[768,512]{1,0:T(8,128)(2,1)S(1)}, u32[]{:S(2)}, u32[]{:S(2)}) collective-permute-start(bf16[768,512]{1,0:T(8,128)(2,1)} %get-tuple-element.59.refs_1_), channel_id=1, source_target_pairs={{0,8},{4,12},{8,16},{12,20},{16,24},{20,28},{1,9},{5,13},{9,17},{1... | collective-permute-start | bytes 2359304 | tf_op jit(solution)/shard_map/ppermute | solution.py:341
  114.2 23.8 %collective-permute-start.16 = (bf16[768,512]{1,0:T(8,128)(2,1)}, bf16[768,512]{1,0:T(8,128)(2,1)}, u32[]{:S(2)}, u32[]{:S(2)}) collective-permute-start(bf16[768,512]{1,0:T(8,128)(2,1)} %get-tuple-element.59.refs_1_), channel_id=1, source_target_pairs={{8,0},{12,4},{16,8},{20,12},{24,16},{28,20},{9,1},{13,5},{17,9},{2... | collective-permute-start | bytes 2359304 | tf_op jit(solution)/shard_map/ppermute | solution.py:345
  116.9 40.6 %collective-permute-start.19 = (bf16[768,384]{1,0:T(8,128)(2,1)}, bf16[768,384]{1,0:T(8,128)(2,1)S(1)}, u32[]{:S(2)}, u32[]{:S(2)}) collective-permute-start(bf16[768,384]{1,0:T(8,128)(2,1)} %get-tuple-element.69.refs_1_), channel_id=1, source_target_pairs={{0,8},{4,12},{8,16},{12,20},{16,24},{20,28},{1,9},{5,13},{9,17},{1... | collective-permute-start | bytes 1769480 | tf_op jit(solution)/shard_map/ppermute | solution.py:341
  121.5 37.1 %collective-permute-start.20 = (bf16[768,384]{1,0:T(8,128)(2,1)}, bf16[768,384]{1,0:T(8,128)(2,1)S(1)}, u32[]{:S(2)}, u32[]{:S(2)}) collective-permute-start(bf16[768,384]{1,0:T(8,128)(2,1)} %get-tuple-element.69.refs_1_), channel_id=1, source_target_pairs={{8,0},{12,4},{16,8},{20,12},{24,16},{28,20},{9,1},{13,5},{17,9},{2... | collective-permute-start | bytes 1769480 | tf_op jit(solution)/shard_map/ppermute | solution.py:345
  122.8 15.2 %copy-start.22 = (bf16[768,384]{1,0:T(8,128)(2,1)S(1)}, bf16[768,384]{1,0:T(8,128)(2,1)}, u32[]{:S(2)}) copy-start(bf16[768,384]{1,0:T(8,128)(2,1)} %get-tuple-element.76.refs_1_) | copy-start | bytes 1769476
  136.8 7.2 %copy-start.19 = (bf16[384,1280]{1,0:T(8,128)(2,1)}, bf16[384,1280]{1,0:T(8,128)(2,1)S(1)}, u32[]{:S(2)}) copy-start(bf16[384,1280]{1,0:T(8,128)(2,1)S(1)} %collective-permute-done.17.refs_10_) | copy-start | bytes 2949124
  136.8 48.3 %collective-permute-start.25 = (bf16[384,1280]{1,0:T(8,128)(2,1)}, bf16[384,1280]{1,0:T(8,128)(2,1)S(1)}, u32[]{:S(2)}, u32[]{:S(2)}) collective-permute-start(bf16[384,1280]{1,0:T(8,128)(2,1)} %get-tuple-element.81), channel_id=1, source_target_pairs={{0,4},{4,0},{8,12},{12,8},{16,20},{20,16},{24,28},{28,24},{1,5},{5... | collective-permute-start | bytes 2949128 | tf_op jit(solution)/shard_map/ppermute | solution.py:337
  138.0 33.6 %collective-permute-start.22 = (bf16[768,384]{1,0:T(8,128)(2,1)S(1)}, bf16[768,384]{1,0:T(8,128)(2,1)S(1)}, u32[]{:S(2)}, u32[]{:S(2)}) collective-permute-start(bf16[768,384]{1,0:T(8,128)(2,1)S(1)} %copy-done.22), channel_id=1, source_target_pairs={{0,8},{4,12},{8,16},{12,20},{16,24},{20,28},{1,9},{5,13},{9,17},{1... | collective-permute-start | bytes 1769480 | tf_op jit(solution)/shard_map/ppermute | solution.py:341
  142.6 29.0 %collective-permute-start.23 = (bf16[768,384]{1,0:T(8,128)(2,1)S(1)}, bf16[768,384]{1,0:T(8,128)(2,1)S(1)}, u32[]{:S(2)}, u32[]{:S(2)}) collective-permute-start(bf16[768,384]{1,0:T(8,128)(2,1)S(1)} %copy-done.22), channel_id=1, source_target_pairs={{8,0},{12,4},{16,8},{20,12},{24,16},{28,20},{9,1},{13,5},{17,9},{2... | collective-permute-start | bytes 1769480 | tf_op jit(solution)/shard_map/ppermute | solution.py:345
  157.6 13.8 %copy-start.8 = (bf16[384,512]{1,0:T(8,128)(2,1)S(1)}, bf16[384,512]{1,0:T(8,128)(2,1)}, u32[]{:S(2)}) copy-start(bf16[384,512]{1,0:T(8,128)(2,1)} %get-tuple-element.64) | copy-start | bytes 1179652
  157.6 13.8 %collective-permute-start.18 = (bf16[384,512]{1,0:T(8,128)(2,1)}, bf16[384,512]{1,0:T(8,128)(2,1)S(1)}, u32[]{:S(2)}, u32[]{:S(2)}) collective-permute-start(bf16[384,512]{1,0:T(8,128)(2,1)} %get-tuple-element.65), channel_id=1, source_target_pairs={{0,4},{4,0},{8,12},{12,8},{16,20},{20,16},{24,28},{28,24},{1,5},{5... | collective-permute-start | bytes 1179656 | tf_op jit(solution)/shard_map/ppermute | solution.py:337
  170.2 16.3 %collective-permute-start.21 = (bf16[384,384]{1,0:T(8,128)(2,1)}, bf16[384,384]{1,0:T(8,128)(2,1)S(1)}, u32[]{:S(2)}, u32[]{:S(2)}) collective-permute-start(bf16[384,384]{1,0:T(8,128)(2,1)} %get-tuple-element.72), channel_id=1, source_target_pairs={{0,4},{4,0},{8,12},{12,8},{16,20},{20,16},{24,28},{28,24},{1,5},{5... | collective-permute-start | bytes 884744 | tf_op jit(solution)/shard_map/ppermute | solution.py:337
  171.5 13.6 %copy-start.6 = (bf16[384,1280]{1,0:T(8,128)(2,1)S(1)}, bf16[384,1280]{1,0:T(8,128)(2,1)}, u32[]{:S(2)}) copy-start(bf16[384,1280]{1,0:T(8,128)(2,1)} %get-tuple-element.57) | copy-start | bytes 2949124
  184.0 7.0 %copy-start.10 = (bf16[384,384]{1,0:T(8,128)(2,1)S(1)}, bf16[384,384]{1,0:T(8,128)(2,1)}, u32[]{:S(2)}) copy-start(bf16[384,384]{1,0:T(8,128)(2,1)} %get-tuple-element.71) | copy-start | bytes 884740
  184.0 7.0 %copy-start.11 = (bf16[384,384]{1,0:T(8,128)(2,1)S(1)}, bf16[384,384]{1,0:T(8,128)(2,1)}, u32[]{:S(2)}) copy-start(bf16[384,384]{1,0:T(8,128)(2,1)} %get-tuple-element.78) | copy-start | bytes 884740
  184.0 7.0 %collective-permute-start.24 = (bf16[384,384]{1,0:T(8,128)(2,1)}, bf16[384,384]{1,0:T(8,128)(2,1)S(1)}, u32[]{:S(2)}, u32[]{:S(2)}) collective-permute-start(bf16[384,384]{1,0:T(8,128)(2,1)} %get-tuple-element.79), channel_id=1, source_target_pairs={{0,4},{4,0},{8,12},{12,8},{16,20},{20,16},{24,28},{28,24},{1,5},{5... | collective-permute-start | bytes 884744 | tf_op jit(solution)/shard_map/ppermute | solution.py:337
  (6 other events, 10.7 us)

commit v2 on v1

--- a/solution.py
+++ b/solution.py
@@ -16,6 +16,7 @@
 SCALE2 = math.log2(math.e) / math.sqrt(HD)
 VMEM = 56 * 1024 * 1024
 BF = jnp.bfloat16
+BRIEF = pl.CostEstimate(flops=0, bytes_accessed=1024, transcendentals=0)
 F32 = jnp.float32
 
 
@@ -110,9 +111,7 @@
         ),
         out_shape=[jax.ShapeDtypeStruct((tokens, width), BF)] * 6,
         compiler_params=pltpu.CompilerParams(vmem_limit_bytes=VMEM),
-        cost_estimate=pl.CostEstimate(
-            flops=0, bytes_accessed=12 * tokens * width * 2, transcendentals=0
-        ),
+        cost_estimate=BRIEF,
         name="norm_pack",
     )(side, totals, gains, *raws)
 
@@ -135,9 +134,7 @@
         out_specs=[pl.BlockSpec((tokens, c1 - c0), lambda i: (i, 0)) for c0, c1 in spans],
         out_shape=[jax.ShapeDtypeStruct((2 * tokens, c1 - c0), BF) for c0, c1 in spans],
         compiler_params=pltpu.CompilerParams(vmem_limit_bytes=VMEM),
-        cost_estimate=pl.CostEstimate(
-            flops=0, bytes_accessed=4 * tokens * width * 2, transcendentals=0
-        ),
+        cost_estimate=BRIEF,
         name="join",
     )(first, second)
 
@@ -191,10 +188,9 @@
     weigh([stage(half, r) for half in range(2) for r in range(readers)], scratch)
 
 
-def self_attention(index, count, k_pieces, v_pieces, q_pieces, first_head, tile, slots):
+def self_attention(index, count, k_pieces, v_pieces, q_pieces, first_head, k_head, heads, tile, slots):
     tokens = q_pieces[0].shape[0]
-    width = k_pieces[0].shape[1]
-    heads = width // HD
+    width = heads * HD
     window = 6 * tokens // tile
 
     def spec(piece, base):
@@ -208,7 +204,7 @@
         grid_spec=pltpu.PrefetchScalarGridSpec(
             num_scalar_prefetch=2,
             grid=(heads,),
-            in_specs=[spec(piece, 0) for piece in k_pieces]
+            in_specs=[spec(piece, k_head) for piece in k_pieces]
             + [spec(piece, first_head) for piece in (*v_pieces, *q_pieces)],
             out_specs=[pl.BlockSpec((tokens, HD), lambda h, *_: (0, h))] * 2,
             scratch_shapes=[
@@ -330,7 +326,7 @@
     shard = lax.axis_index("frame")
     side = shard % 2
     pair = shard // 2
-    cuts = [0, (2 * heads + 4) // 5, (7 * heads + 9) // 10, heads]
+    cuts = [0, (heads + 1) // 2, heads]
     chunks = [(a * HD, b * HD) for a, b in zip(cuts, cuts[1:])]
 
     def partner(value):
@@ -395,12 +391,12 @@
 
     keep_q, keep_k, keep_cq, send_q, send_k, send_cq = pack(
         jnp.reshape(side, (1,)),
-        after(totals[:, : 3 * tokens].reshape(2, 3, 1, tokens), v_got, got_meta),
+        totals[:, : 3 * tokens].reshape(2, 3, 1, tokens),
         jnp.stack([q_gain, k_gain, cross_q_gain]),
         (q_raw, k_raw, cross_q_raw),
     )
-    got_cq = partner(after(send_cq, v_up, v_down))
-    got_k = partner(after(send_k, text_got, v_got_up, v_got_down))
+    got_k = partner(after(send_k, text_got, v_up, v_down))
+    got_cq = partner(after(send_cq, got_k, got_meta))
     got_q = partner(after(send_q, got_cq))
     cross_pieces = [keep_cq, got_cq]
     q_pieces = [keep_q, got_q]
@@ -417,23 +413,27 @@
     joined_k = join(keep_k, got_k, chunks)
     k_pieces = []
     for number, own in enumerate(joined_k):
-        if number < 2:
-            own = after(own, *text[max(0, 1 - number) : len(text) - max(0, 1 - number)])
-        else:
-            own = after(own, *k_pieces[number - 2])
+        if number == 0:
+            own = after(own, v_got_up, v_got_down)
+        own = after(own, *text[max(0, 1 - number) : len(text) - max(0, 1 - number)])
         k_pieces.append([up(own), own, down(own)])
 
     cross_keep, cross_send = cross_attention(place, text, cross_pieces, text_total, order)
     cross_got = partner(after(cross_send, got_q))
     self_keep, self_got = [], []
-    for number, chunk in enumerate(chunks):
+    calls = [(0, 0, cuts[1]), (1, cuts[1], heads)]
+    for order_of_call, (number, c0, c1) in enumerate(calls):
+        waits = [cross_keep, *self_keep]
+        waits += [cross_got, *self_got][:order_of_call]
         out_keep, out_send = self_attention(
             index,
             count,
-            [after(k, cross_keep, *self_keep) for k in k_pieces[number]],
+            [after(k, *waits) for k in k_pieces[number]],
             v_pieces,
             q_pieces,
-            chunk[0] // HD,
+            c0,
+            c0 - cuts[number],
+            c1 - c0,
             tile,
             slots,
         )

time: 195 us -> 197 us (1.010)
  waiting for transfers between devices: 50.7 us -> 64.4 us
  starting transfers between devices: 54.2 us -> 49 us
  Pallas kernels: 59.5 us -> 56.7 us
  local copies, waits for them, and re-layouts: 8.95 us -> 6.39 us
    ppermute x8 -> x7, waiting for transfers between devices: 15.4 us -> 34.9 us  [down(): return lax.ppermute(value, 'frame', moves)]
    ppermute x8 -> x7, waiting for transfers between devices: 6.17 us -> 0.02 us  [up(): return lax.ppermute(value, 'frame', moves)]
    ppermute x8 -> x7, starting transfers between devices: 32.6 us -> 29 us  [up(): return lax.ppermute(value, 'frame', moves)]
    pallas_call x3 -> x2, Pallas kernels: 35.1 us -> 32.5 us  [self_attention(): pl.pallas_call(functools.partial(self_kernel, tile=tile, slots=slots, n_k...]
    unnamed x56 -> x48, local copies, waits for them, and re-layouts: 3.59 us -> 1.05 us
    ppermute x8 -> x7, starting transfers between devices: 10.5 us -> 9.01 us  [down(): return lax.ppermute(value, 'frame', moves)]
    ppermute x10 -> x9, waiting for transfers between devices: 29.1 us -> 29.5 us  [partner(): return lax.ppermute(value, 'frame', [(i, i ^ 1) for i in range(shards)])]
    ppermute x10 -> x9, starting transfers between devices: 11.2 us -> 11 us  [partner(): return lax.ppermute(value, 'frame', [(i, i ^ 1) for i in range(shards)])]
  transfers between devices with their start and end apart: 26 -> 23, of which waited for: 11 -> 5; matrix products, arithmetic and copies ran while one was open for 4% -> 4% of each run, Pallas kernels for 31% -> 29%
where the time goes in v2:
time: 197 us; the launch traced here: 196 us
  waiting for transfers between devices  64.4 us (33%)
  Pallas kernels  56.7 us (29%)
  starting transfers between devices  49 us (25%)
  blocking collectives  11.1 us (6%)
  other arithmetic  7.04 us (4%)
  local copies, waits for them, and re-layouts  6.39 us (3%)
    ppermute x7, waiting for transfers between devices, down(): return lax.ppermute(value, 'frame', moves)  34.9 us
    pallas_call x2, Pallas kernels, self_attention(): pl.pallas_call(functools.partial(self_kernel, tile=tile, slots=slots, n_k...  32.5 us
    ppermute x9, waiting for transfers between devices, partner(): return lax.ppermute(value, 'frame', [(i, i ^ 1) for i in range(shards)])  29.5 us
    ppermute x7, starting transfers between devices, up(): return lax.ppermute(value, 'frame', moves)  29 us
    pallas_call x1, Pallas kernels, cross_attention(): pl.pallas_call(functools.partial(cross_kernel, n_text=len(text), text_tot...  13.9 us
    psum x1, blocking collectives, body(): totals = lax.psum(sums, 'head')  11.1 us
    ppermute x9, starting transfers between devices, partner(): return lax.ppermute(value, 'frame', [(i, i ^ 1) for i in range(shards)])  11 us
    ppermute x7, starting transfers between devices, down(): return lax.ppermute(value, 'frame', moves)  9.01 us
  transfers between devices with their start and end apart: 23, of which 5 were waited for; matrix products, arithmetic and copies ran while one was open for 4% of the time, Pallas kernels for 29%

profile of v2, /device:TPU:0, one launch (start us, length us, event | category | flops | bytes accessed | tf_op | source)
XLA Modules:
  0.0 195.7 jit_solution(6827010995506280855)
XLA Ops:
  0.7 2.7 %dynamic-slice_bitcast_fusion = (bf16[384,1280]{1,0:T(8,128)(2,1)}, bf16[384,1280]{1,0:T(8,128)(2,1)S(1)}) fusion(bf16[2,384,1280]{2,1,0:T(8,128)(2,1)} %param.15, s32[]{:T(128)S(6)} %select_n.58, s32[]{:T(128)S(6)} %select_n.57), kind=kLoop, calls=%fused_computation.5 | loop fusion | bytes 3932168 | tf_op jit(solution)/shard_map/jit(dynamic_index_in_dim)/squeeze | solution.py:347
  3.4 5.2 %collective-permute-start.3 = (bf16[384,1280]{1,0:T(8,128)(2,1)S(1)}, bf16[384,1280]{1,0:T(8,128)(2,1)S(1)}, u32[]{:S(2)}, u32[]{:S(2)}) collective-permute-start(bf16[384,1280]{1,0:T(8,128)(2,1)S(1)} %get-tuple-element.69.refs_5_), channel_id=1, source_target_pairs={{0,8},{4,12},{8,16},{12,20},{16,24},{20,28},{1,9},{5,13},{9,17},{1... | collective-permute-start | bytes 2949128 | tf_op jit(solution)/shard_map/ppermute | solution.py:337
  8.7 1.3 collective-permute-start.4
  10.0 1.6 collective-permute-start.1
  11.6 0.5 multiply_reduce_fusion.2
  12.2 0.8 multiply_reduce_fusion
  13.1 11.1 %psum.7 = f32[2,1216]{1,0:T(2,128)S(1)} all-reduce(f32[2,1216]{1,0:T(2,128)S(1)} %pad_maximum_fusion.3), channel_id=1, replica_groups=mesh['frame'=8,'head'=4] {'head'}, use_global_device_ids=true, to_apply=%region_4.5 | all-reduce | flops 2432 | bytes 19456 | tf_op jit(solution)/shard_map/psum | solution.py:371
  24.2 0.1 fusion
  24.5 9.1 %collective-permute-done.1.refs_6_ = bf16[384,1280]{1,0:T(8,128)(2,1)} collective-permute-done((bf16[384,1280]{1,0:T(8,128)(2,1)}, bf16[384,1280]{1,0:T(8,128)(2,1)}, u32[]{:S(2)}, u32[]{:S(2)}) %collective-permute-start.1) | collective-permute-done | bytes 983072 | tf_op jit(solution)/shard_map/ppermute | solution.py:333
  33.6 1.5 collective-permute-start.2
  35.1 0.6 reshape.28.totals
  35.8 0.6 pad_maximum_fusion.2.gains
  36.4 7.5 %norm_pack.1 = (bf16[384,1280]{1,0:T(8,128)(2,1)}, bf16[384,1280]{1,0:T(8,128)(2,1)}, bf16[384,1280]{1,0:T(8,128)(2,1)}, bf16[384,1280]{1,0:T(8,128)(2,1)}, bf16...) custom-call(s32[1]{0:T(128)} %bitcast.1.side, f32[2,3,1,384]{3,2,1,0:T(1,128)} %reshape.28.totals, ...), custom_call_target="tpu_custom_call" | custom-call | bytes 1024 | tf_op jit(solution)/shard_map/norm_pack/pallas_call | solution.py:104
  43.9 0.6 collective-permute-start.5
  44.6 4.3 %collective-permute-start.8 = (bf16[2,128,1280]{2,1,0:T(8,128)(2,1)S(1)}, bf16[2,128,1280]{2,1,0:T(8,128)(2,1)S(1)}, u32[]{:S(2)}, u32[]{:S(2)}) collective-permute-start(bf16[2,128,1280]{2,1,0:T(8,128)(2,1)S(1)} %pad_maximum_fusion.1.refs_3_), channel_id=1, source_target_pairs={{0,8},{4,12},{8,16},{12,20},{16,24},{20,28},{1,9},{5,13},{9,17},{1... | collective-permute-start | bytes 1966088 | tf_op jit(solution)/shard_map/ppermute | solution.py:337
  48.9 1.3 collective-permute-start.10
  50.3 1.5 collective-permute-start
  51.9 14.4 %collective-permute-done = s32[3,15]{1,0:T(4,128)S(1)} collective-permute-done((s32[3,15]{1,0:T(4,128)S(1)}, s32[3,15]{1,0:T(4,128)S(1)}, u32[]{:S(2)}, u32[]{:S(2)}) %collective-permute-start) | collective-permute-done | bytes 212 | tf_op jit(solution)/shard_map/ppermute | solution.py:333
  66.3 0.5 collective-permute-start.15
  66.8 4.0 %collective-permute-start.6 = (bf16[384,1280]{1,0:T(8,128)(2,1)}, bf16[384,1280]{1,0:T(8,128)(2,1)S(1)}, u32[]{:S(2)}, u32[]{:S(2)}) collective-permute-start(bf16[384,1280]{1,0:T(8,128)(2,1)} %collective-permute-done.1.refs_6_), channel_id=1, source_target_pairs={{0,8},{4,12},{8,16},{12,20},{16,24},{20,28},{1,9},{5,13},{9,17},{1... | collective-permute-start | bytes 2949128 | tf_op jit(solution)/shard_map/ppermute | solution.py:337
  70.8 1.3 collective-permute-start.7
  72.1 1.5 collective-permute-start.9
  73.6 1.3 collective-permute-start.11
  74.9 1.5 collective-permute-start.13
  76.5 31.0 %collective-permute-done.11.refs_5_ = bf16[2,128,1280]{2,1,0:T(8,128)(2,1)} collective-permute-done((bf16[2,128,1280]{2,1,0:T(8,128)(2,1)}, bf16[2,128,1280]{2,1,0:T(8,128)(2,1)}, u32[]{:S(2)}, u32[]{:S(2)}) %collective-permute-start.11) | collective-permute-done | bytes 655392 | tf_op jit(solution)/shard_map/ppermute | solution.py:341
  107.4 1.3 collective-permute-start.14
  108.7 1.6 collective-permute-start.17
  110.3 2.9 %join.1 = (bf16[768,640]{1,0:T(8,128)(2,1)}, bf16[768,640]{1,0:T(8,128)(2,1)}) custom-call(bf16[384,1280]{1,0:T(8,128)(2,1)} %get-tuple-element.39.first, bf16[384,1280]{1,0:T(8,128)(2,1)} %copy-done.5), custom_call_target="tpu_custom_call" | custom-call | bytes 1024 | tf_op jit(solution)/shard_map/join/pallas_call | solution.py:130
  113.2 1.3 collective-permute-start.16
  114.5 6.9 %collective-permute-start.12 = (bf16[768,640]{1,0:T(8,128)(2,1)}, bf16[768,640]{1,0:T(8,128)(2,1)}, u32[]{:S(2)}, u32[]{:S(2)}) collective-permute-start(bf16[768,640]{1,0:T(8,128)(2,1)} %get-tuple-element.52.refs_1_), channel_id=1, source_target_pairs={{0,8},{4,12},{8,16},{12,20},{16,24},{20,28},{1,9},{5,13},{9,17},{1... | collective-permute-start | bytes 2949128 | tf_op jit(solution)/shard_map/ppermute | solution.py:337
  121.4 0.6 dynamic_slice.21
  122.0 1.3 pad_add_fusion.2.place
  123.4 3.9 %collective-permute-done.14.refs_6_ = bf16[2,128,1280]{2,1,0:T(8,128)(2,1)} collective-permute-done((bf16[2,128,1280]{2,1,0:T(8,128)(2,1)}, bf16[2,128,1280]{2,1,0:T(8,128)(2,1)}, u32[]{:S(2)}, u32[]{:S(2)}) %collective-permute-start.14) | collective-permute-done | bytes 655392 | tf_op jit(solution)/shard_map/ppermute | solution.py:341
  127.3 1.3 collective-permute-start.21
  128.6 5.5 %collective-permute-start.19 = (bf16[768,640]{1,0:T(8,128)(2,1)}, bf16[768,640]{1,0:T(8,128)(2,1)}, u32[]{:S(2)}, u32[]{:S(2)}) collective-permute-start(bf16[768,640]{1,0:T(8,128)(2,1)} %get-tuple-element.64.refs_1_), channel_id=1, source_target_pairs={{0,8},{4,12},{8,16},{12,20},{16,24},{20,28},{1,9},{5,13},{9,17},{1... | collective-permute-start | bytes 2949128 | tf_op jit(solution)/shard_map/ppermute | solution.py:337
  134.1 13.9 %cross_attention.1 = (bf16[384,1280]{1,0:T(8,128)(2,1)}, bf16[384,1280]{1,0:T(8,128)(2,1)}) custom-call(s32[3]{0:T(128)} %pad_add_fusion.2.place, bf16[2,128,1280]{2,1,0:T(8,128)(2,1)} %collective-permute-done.13.refs_0_, bf16[2,128,1280]{2,1,0:T(8,128)(2,1)} %collective-permute-done.9.refs_1_, bf16[2,128,1280]{2,1,0:T(8,128)(2,1)} %copy-done.22, ...), custom_call_target="tpu_custom_call" | custom-call | flops 4026531840 | bytes 8519680 | tf_op jit(solution)/shard_map/cross_attention/pallas_call | solution.py:280
  148.0 1.6 collective-permute-start.20
  149.6 0.6 reshape.26.index
  150.2 0.7 slice_reduce_fusion.count
  150.9 0.9 copy-done.21
  151.8 16.1 %self_attention.2 = (bf16[384,640]{1,0:T(8,128)(2,1)}, bf16[384,640]{1,0:T(8,128)(2,1)}) custom-call(s32[84]{0:T(128)} %reshape.26.index, s32[6]{0:T(128)} %slice_reduce_fusion.count, bf16[768,640]{1,0:T(8,128)(2,1)} %collective-permute-done.12.refs_0_, bf16[768,640]{1,0:T(8,128)(2,1)} %get-tuple-element.52.refs_1_, bf16[768,640]{1,0:T(8,128)(2,1)} %copy-done.21, ...), custom_call_target="tpu_custom_call" | custom-call | flops 7046430720 | bytes 7864320 | tf_op jit(solution)/shard_map/self_attention/pallas_call | solution.py:200
  168.0 0.6 collective-permute-start.18
  168.6 16.4 %self_attention.3 = (bf16[384,640]{1,0:T(8,128)(2,1)}, bf16[384,640]{1,0:T(8,128)(2,1)}) custom-call(s32[84]{0:T(128)} %reshape.26.index, s32[6]{0:T(128)} %slice_reduce_fusion.count, bf16[768,640]{1,0:T(8,128)(2,1)} %collective-permute-done.19.refs_0_, bf16[768,640]{1,0:T(8,128)(2,1)} %get-tuple-element.64.refs_1_, ...), custom_call_target="tpu_custom_call" | custom-call | flops 7046430720 | bytes 7864320 | tf_op jit(solution)/shard_map/self_attention/pallas_call | solution.py:200
  184.9 1.6 collective-permute-start.22
  186.5 1.5 broadcast_select_fusion
  188.0 6.0 %collective-permute-done.22 = bf16[384,640]{1,0:T(8,128)(2,1)S(1)} collective-permute-done((bf16[384,640]{1,0:T(8,128)(2,1)}, bf16[384,640]{1,0:T(8,128)(2,1)S(1)}, u32[]{:S(2)}, u32[]{:S(2)}) %collective-permute-start.22) | collective-permute-done | bytes 491552 | tf_op jit(solution)/shard_map/ppermute | solution.py:333
  194.0 0.3 broadcast_select_fusion.2
  194.3 1.4 pad_maximum_fusion
  (79 shorter events, 0.7 us)
Async XLA Ops:
  0.7 10.9 %copy-start.2 = (bf16[2,384,1280]{2,1,0:T(8,128)(2,1)S(1)}, bf16[2,384,1280]{2,1,0:T(8,128)(2,1)}, u32[]{:S(2)}) copy-start(bf16[2,384,1280]{2,1,0:T(8,128)(2,1)} %refs_0_.1) | copy-start | bytes 5898244
  0.7 11.3 %copy-start.3 = (bf16[2,64,1280]{2,1,0:T(8,128)(2,1)S(1)}, bf16[2,64,1280]{2,1,0:T(8,128)(2,1)}, u32[]{:S(2)}) copy-start(bf16[2,64,1280]{2,1,0:T(8,128)(2,1)} %param.17) | copy-start | bytes 983044
  0.7 11.5 %copy-start.1 = (bf16[2,384,1280]{2,1,0:T(8,128)(2,1)S(1)}, bf16[2,384,1280]{2,1,0:T(8,128)(2,1)}, u32[]{:S(2)}) copy-start(bf16[2,384,1280]{2,1,0:T(8,128)(2,1)} %refs_1_.1) | copy-start | bytes 5898244
  3.4 9.6 %copy-start.4 = (bf16[384,1280]{1,0:T(8,128)(2,1)}, bf16[384,1280]{1,0:T(8,128)(2,1)S(1)}, u32[]{:S(2)}) copy-start(bf16[384,1280]{1,0:T(8,128)(2,1)S(1)} %get-tuple-element.69.refs_5_) | copy-start | bytes 2949124
  3.4 8.8 %copy-start = (bf16[2,384,1280]{2,1,0:T(8,128)(2,1)S(1)}, bf16[2,384,1280]{2,1,0:T(8,128)(2,1)}, u32[]{:S(2)}) copy-start(bf16[2,384,1280]{2,1,0:T(8,128)(2,1)} %refs_2_.1) | copy-start | bytes 5898244
  3.4 40.5 %collective-permute-start.3 = (bf16[384,1280]{1,0:T(8,128)(2,1)S(1)}, bf16[384,1280]{1,0:T(8,128)(2,1)S(1)}, u32[]{:S(2)}, u32[]{:S(2)}) collective-permute-start(bf16[384,1280]{1,0:T(8,128)(2,1)S(1)} %get-tuple-element.69.refs_5_), channel_id=1, source_target_pairs={{0,8},{4,12},{8,16},{12,20},{16,24},{20,28},{1,9},{5,13},{9,17},{1... | collective-permute-start | bytes 2949128 | tf_op jit(solution)/shard_map/ppermute | solution.py:337
  8.7 35.2 %collective-permute-start.4 = (bf16[384,1280]{1,0:T(8,128)(2,1)S(1)}, bf16[384,1280]{1,0:T(8,128)(2,1)}, u32[]{:S(2)}, u32[]{:S(2)}) collective-permute-start(bf16[384,1280]{1,0:T(8,128)(2,1)S(1)} %get-tuple-element.69.refs_5_), channel_id=1, source_target_pairs={{8,0},{12,4},{16,8},{20,12},{24,16},{28,20},{9,1},{13,5},{17,9},{2... | collective-permute-start | bytes 2949128 | tf_op jit(solution)/shard_map/ppermute | solution.py:341
  10.0 23.6 %collective-permute-start.1 = (bf16[384,1280]{1,0:T(8,128)(2,1)}, bf16[384,1280]{1,0:T(8,128)(2,1)}, u32[]{:S(2)}, u32[]{:S(2)}) collective-permute-start(bf16[384,1280]{1,0:T(8,128)(2,1)} %get-tuple-element.68), channel_id=1, source_target_pairs={{0,4},{4,0},{8,12},{12,8},{16,20},{20,16},{24,28},{28,24},{1,5},{5... | collective-permute-start | bytes 2949128 | tf_op jit(solution)/shard_map/ppermute | solution.py:333
  12.2 12.0 %copy-start.15 = (f32[1280]{0:T(1024)S(1)}, f32[1280]{0:T(1024)}, u32[]{:S(2)}) copy-start(f32[1280]{0:T(1024)} %param.22) | copy-start | bytes 15364
  12.2 12.2 %copy-start.10 = (bf16[2,64,1280]{2,1,0:T(8,128)(2,1)S(1)}, bf16[2,64,1280]{2,1,0:T(8,128)(2,1)}, u32[]{:S(2)}) copy-start(bf16[2,64,1280]{2,1,0:T(8,128)(2,1)} %param.18) | copy-start | bytes 983044
  13.1 22.7 %copy-start.12 = (f32[1280]{0:T(1024)S(1)}, f32[1280]{0:T(1024)}, u32[]{:S(2)}) copy-start(f32[1280]{0:T(1024)} %param.19) | copy-start | bytes 15364
  13.1 22.7 %copy-start.13 = (f32[1280]{0:T(1024)S(1)}, f32[1280]{0:T(1024)}, u32[]{:S(2)}) copy-start(f32[1280]{0:T(1024)} %param.20) | copy-start | bytes 15364
  13.1 22.7 %copy-start.14 = (f32[1280]{0:T(1024)S(1)}, f32[1280]{0:T(1024)}, u32[]{:S(2)}) copy-start(f32[1280]{0:T(1024)} %param.21) | copy-start | bytes 15364
  33.6 10.4 %collective-permute-start.2 = (bf16[2,64,1280]{2,1,0:T(8,128)(2,1)S(1)}, bf16[2,64,1280]{2,1,0:T(8,128)(2,1)S(1)}, u32[]{:S(2)}, u32[]{:S(2)}) collective-permute-start(bf16[2,64,1280]{2,1,0:T(8,128)(2,1)S(1)} %get-tuple-element.41), channel_id=1, source_target_pairs={{0,4},{4,0},{8,12},{12,8},{16,20},{20,16},{24,28},{28,24},{1,5},{5... | collective-permute-start | bytes 983048 | tf_op jit(solution)/shard_map/ppermute | solution.py:333
  36.4 13.8 %copy-start.16 = (s32[3]{0:T(128)S(1)}, s32[3]{0:T(128)}, u32[]{:S(2)}) copy-start(s32[3]{0:T(128)} %param.24) | copy-start | bytes 40
  36.4 13.9 %copy-start.11 = (s32[3,14]{1,0:T(4,128)S(1)}, s32[3,14]{1,0:T(4,128)}, u32[]{:S(2)}) copy-start(s32[3,14]{1,0:T(4,128)} %param.23) | copy-start | bytes 508
  43.9 77.5 %copy-start.23 = (s32[2]{0:T(128)S(1)}, s32[2]{0:T(128)}, u32[]{:S(2)}) copy-start(s32[2]{0:T(128)} %param.25) | copy-start | bytes 28
  43.9 104.1 %copy-start.17 = (bf16[384,1280]{1,0:T(8,128)(2,1)}, bf16[384,1280]{1,0:T(8,128)(2,1)S(1)}, u32[]{:S(2)}) copy-start(bf16[384,1280]{1,0:T(8,128)(2,1)S(1)} %collective-permute-done.3.refs_3_) | copy-start | bytes 2949124
  43.9 22.3 %collective-permute-start.5 = (bf16[384,1280]{1,0:T(8,128)(2,1)}, bf16[384,1280]{1,0:T(8,128)(2,1)S(1)}, u32[]{:S(2)}, u32[]{:S(2)}) collective-permute-start(bf16[384,1280]{1,0:T(8,128)(2,1)} %get-tuple-element.42), channel_id=1, source_target_pairs={{0,4},{4,0},{8,12},{12,8},{16,20},{20,16},{24,28},{28,24},{1,5},{5... | collective-permute-start | bytes 2949128 | tf_op jit(solution)/shard_map/ppermute | solution.py:333
  44.5 89.5 %copy-start.7 = (bf16[2,128,1280]{2,1,0:T(8,128)(2,1)}, bf16[2,128,1280]{2,1,0:T(8,128)(2,1)S(1)}, u32[]{:S(2)}) copy-start(bf16[2,128,1280]{2,1,0:T(8,128)(2,1)S(1)} %pad_maximum_fusion.1.refs_3_) | copy-start | bytes 1966084
  44.6 27.6 %collective-permute-start.8 = (bf16[2,128,1280]{2,1,0:T(8,128)(2,1)S(1)}, bf16[2,128,1280]{2,1,0:T(8,128)(2,1)S(1)}, u32[]{:S(2)}, u32[]{:S(2)}) collective-permute-start(bf16[2,128,1280]{2,1,0:T(8,128)(2,1)S(1)} %pad_maximum_fusion.1.refs_3_), channel_id=1, source_target_pairs={{0,8},{4,12},{8,16},{12,20},{16,24},{20,28},{1,9},{5,13},{9,17},{1... | collective-permute-start | bytes 1966088 | tf_op jit(solution)/shard_map/ppermute | solution.py:337
  48.9 24.8 %collective-permute-start.10 = (bf16[2,128,1280]{2,1,0:T(8,128)(2,1)S(1)}, bf16[2,128,1280]{2,1,0:T(8,128)(2,1)}, u32[]{:S(2)}, u32[]{:S(2)}) collective-permute-start(bf16[2,128,1280]{2,1,0:T(8,128)(2,1)S(1)} %pad_maximum_fusion.1.refs_3_), channel_id=1, source_target_pairs={{8,0},{12,4},{16,8},{20,12},{24,16},{28,20},{9,1},{13,5},{17,9},{2... | collective-permute-start | bytes 1966088 | tf_op jit(solution)/shard_map/ppermute | solution.py:341
  50.3 15.9 %collective-permute-start = (s32[3,15]{1,0:T(4,128)S(1)}, s32[3,15]{1,0:T(4,128)S(1)}, u32[]{:S(2)}, u32[]{:S(2)}) collective-permute-start(s32[3,15]{1,0:T(4,128)S(1)} %pad_add_fusion.1), channel_id=1, source_target_pairs={{0,4},{4,0},{8,12},{12,8},{16,20},{20,16},{24,28},{28,24},{1,5},{5... | collective-permute-start | bytes 548 | tf_op jit(solution)/shard_map/ppermute | solution.py:333
  66.3 44.0 %copy-start.5 = (bf16[384,1280]{1,0:T(8,128)(2,1)}, bf16[384,1280]{1,0:T(8,128)(2,1)S(1)}, u32[]{:S(2)}) copy-start(bf16[384,1280]{1,0:T(8,128)(2,1)S(1)} %collective-permute-done.5.second) | copy-start | bytes 2949124
  66.3 42.4 %collective-permute-start.15 = (bf16[384,1280]{1,0:T(8,128)(2,1)}, bf16[384,1280]{1,0:T(8,128)(2,1)S(1)}, u32[]{:S(2)}, u32[]{:S(2)}) collective-permute-start(bf16[384,1280]{1,0:T(8,128)(2,1)} %get-tuple-element.49), channel_id=1, source_target_pairs={{0,4},{4,0},{8,12},{12,8},{16,20},{20,16},{24,28},{28,24},{1,5},{5... | collective-permute-start | bytes 2949128 | tf_op jit(solution)/shard_map/ppermute | solution.py:333
  66.8 46.4 %collective-permute-start.6 = (bf16[384,1280]{1,0:T(8,128)(2,1)}, bf16[384,1280]{1,0:T(8,128)(2,1)S(1)}, u32[]{:S(2)}, u32[]{:S(2)}) collective-permute-start(bf16[384,1280]{1,0:T(8,128)(2,1)} %collective-permute-done.1.refs_6_), channel_id=1, source_target_pairs={{0,8},{4,12},{8,16},{12,20},{16,24},{20,28},{1,9},{5,13},{9,17},{1... | collective-permute-start | bytes 2949128 | tf_op jit(solution)/shard_map/ppermute | solution.py:337
  70.8 42.4 %collective-permute-start.7 = (bf16[384,1280]{1,0:T(8,128)(2,1)}, bf16[384,1280]{1,0:T(8,128)(2,1)S(1)}, u32[]{:S(2)}, u32[]{:S(2)}) collective-permute-start(bf16[384,1280]{1,0:T(8,128)(2,1)} %collective-permute-done.1.refs_6_), channel_id=1, source_target_pairs={{8,0},{12,4},{16,8},{20,12},{24,16},{28,20},{9,1},{13,5},{17,9},{2... | collective-permute-start | bytes 2949128 | tf_op jit(solution)/shard_map/ppermute | solution.py:341
  72.1 49.9 %copy-start.22 = (bf16[2,128,1280]{2,1,0:T(8,128)(2,1)}, bf16[2,128,1280]{2,1,0:T(8,128)(2,1)S(1)}, u32[]{:S(2)}) copy-start(bf16[2,128,1280]{2,1,0:T(8,128)(2,1)S(1)} %collective-permute-done.8.refs_2_) | copy-start | bytes 1966084
  72.1 2.8 %collective-permute-start.9 = (bf16[2,128,1280]{2,1,0:T(8,128)(2,1)S(1)}, bf16[2,128,1280]{2,1,0:T(8,128)(2,1)}, u32[]{:S(2)}, u32[]{:S(2)}) collective-permute-start(bf16[2,128,1280]{2,1,0:T(8,128)(2,1)S(1)} %collective-permute-done.8.refs_2_), channel_id=1, source_target_pairs={{8,16},{12,20},{16,24},{20,28},{9,17},{13,21},{17,25},{21,29},{10,... | collective-permute-start | bytes 1966088 | tf_op jit(solution)/shard_map/ppermute | solution.py:337
  73.6 33.8 %collective-permute-start.11 = (bf16[2,128,1280]{2,1,0:T(8,128)(2,1)}, bf16[2,128,1280]{2,1,0:T(8,128)(2,1)}, u32[]{:S(2)}, u32[]{:S(2)}) collective-permute-start(bf16[2,128,1280]{2,1,0:T(8,128)(2,1)} %collective-permute-done.10.refs_4_), channel_id=1, source_target_pairs={{8,0},{12,4},{16,8},{20,12},{9,1},{13,5},{17,9},{21,13},{10,2},{14... | collective-permute-start | bytes 1966088 | tf_op jit(solution)/shard_map/ppermute | solution.py:341
  74.9 48.5 %collective-permute-start.13 = (bf16[2,128,1280]{2,1,0:T(8,128)(2,1)}, bf16[2,128,1280]{2,1,0:T(8,128)(2,1)}, u32[]{:S(2)}, u32[]{:S(2)}) collective-permute-start(bf16[2,128,1280]{2,1,0:T(8,128)(2,1)} %collective-permute-done.9.refs_1_), channel_id=1, source_target_pairs={{16,24},{20,28},{17,25},{21,29},{18,26},{22,30},{19,27},{23,31}} | collective-permute-start | bytes 1966088 | tf_op jit(solution)/shard_map/ppermute | solution.py:337
  107.4 19.9 %collective-permute-start.14 = (bf16[2,128,1280]{2,1,0:T(8,128)(2,1)}, bf16[2,128,1280]{2,1,0:T(8,128)(2,1)}, u32[]{:S(2)}, u32[]{:S(2)}) collective-permute-start(bf16[2,128,1280]{2,1,0:T(8,128)(2,1)} %collective-permute-done.11.refs_5_), channel_id=1, source_target_pairs={{8,0},{12,4},{9,1},{13,5},{10,2},{14,6},{11,3},{15,7}} | collective-permute-start | bytes 1966088 | tf_op jit(solution)/shard_map/ppermute | solution.py:341
  108.7 12.7 %copy-start.20 = (bf16[384,1280]{1,0:T(8,128)(2,1)}, bf16[384,1280]{1,0:T(8,128)(2,1)S(1)}, u32[]{:S(2)}) copy-start(bf16[384,1280]{1,0:T(8,128)(2,1)S(1)} %collective-permute-done.15.refs_8_) | copy-start | bytes 2949124
  108.7 39.3 %collective-permute-start.17 = (bf16[384,1280]{1,0:T(8,128)(2,1)}, bf16[384,1280]{1,0:T(8,128)(2,1)}, u32[]{:S(2)}, u32[]{:S(2)}) collective-permute-start(bf16[384,1280]{1,0:T(8,128)(2,1)} %get-tuple-element.56), channel_id=1, source_target_pairs={{0,4},{4,0},{8,12},{12,8},{16,20},{20,16},{24,28},{28,24},{1,5},{5... | collective-permute-start | bytes 2949128 | tf_op jit(solution)/shard_map/ppermute | solution.py:333
  113.2 1.3 copy-start.18
  113.2 8.2 %copy-start.19 = (bf16[384,1280]{1,0:T(8,128)(2,1)}, bf16[384,1280]{1,0:T(8,128)(2,1)S(1)}, u32[]{:S(2)}) copy-start(bf16[384,1280]{1,0:T(8,128)(2,1)S(1)} %collective-permute-done.7.refs_8_) | copy-start | bytes 2949124
  113.2 37.7 %collective-permute-start.16 = (bf16[768,640]{1,0:T(8,128)(2,1)}, bf16[768,640]{1,0:T(8,128)(2,1)S(1)}, u32[]{:S(2)}, u32[]{:S(2)}) collective-permute-start(bf16[768,640]{1,0:T(8,128)(2,1)} %get-tuple-element.52.refs_1_), channel_id=1, source_target_pairs={{8,0},{12,4},{16,8},{20,12},{24,16},{28,20},{9,1},{13,5},{17,9},{2... | collective-permute-start | bytes 2949128 | tf_op jit(solution)/shard_map/ppermute | solution.py:341
  114.5 36.4 %collective-permute-start.12 = (bf16[768,640]{1,0:T(8,128)(2,1)}, bf16[768,640]{1,0:T(8,128)(2,1)}, u32[]{:S(2)}, u32[]{:S(2)}) collective-permute-start(bf16[768,640]{1,0:T(8,128)(2,1)} %get-tuple-element.52.refs_1_), channel_id=1, source_target_pairs={{0,8},{4,12},{8,16},{12,20},{16,24},{20,28},{1,9},{5,13},{9,17},{1... | collective-permute-start | bytes 2949128 | tf_op jit(solution)/shard_map/ppermute | solution.py:337
  127.3 41.3 %collective-permute-start.21 = (bf16[768,640]{1,0:T(8,128)(2,1)}, bf16[768,640]{1,0:T(8,128)(2,1)}, u32[]{:S(2)}, u32[]{:S(2)}) collective-permute-start(bf16[768,640]{1,0:T(8,128)(2,1)} %get-tuple-element.64.refs_1_), channel_id=1, source_target_pairs={{8,0},{12,4},{16,8},{20,12},{24,16},{28,20},{9,1},{13,5},{17,9},{2... | collective-permute-start | bytes 2949128 | tf_op jit(solution)/shard_map/ppermute | solution.py:341
  128.6 40.0 %collective-permute-start.19 = (bf16[768,640]{1,0:T(8,128)(2,1)}, bf16[768,640]{1,0:T(8,128)(2,1)}, u32[]{:S(2)}, u32[]{:S(2)}) collective-permute-start(bf16[768,640]{1,0:T(8,128)(2,1)} %get-tuple-element.64.refs_1_), channel_id=1, source_target_pairs={{0,8},{4,12},{8,16},{12,20},{16,24},{20,28},{1,9},{5,13},{9,17},{1... | collective-permute-start | bytes 2949128 | tf_op jit(solution)/shard_map/ppermute | solution.py:337
  148.0 20.6 %collective-permute-start.20 = (bf16[384,1280]{1,0:T(8,128)(2,1)}, bf16[384,1280]{1,0:T(8,128)(2,1)S(1)}, u32[]{:S(2)}, u32[]{:S(2)}) collective-permute-start(bf16[384,1280]{1,0:T(8,128)(2,1)} %get-tuple-element.62), channel_id=1, source_target_pairs={{0,4},{4,0},{8,12},{12,8},{16,20},{20,16},{24,28},{28,24},{1,5},{5... | collective-permute-start | bytes 2949128 | tf_op jit(solution)/shard_map/ppermute | solution.py:333
  150.9 0.9 copy-start.21
  168.0 20.1 %collective-permute-start.18 = (bf16[384,640]{1,0:T(8,128)(2,1)}, bf16[384,640]{1,0:T(8,128)(2,1)S(1)}, u32[]{:S(2)}, u32[]{:S(2)}) collective-permute-start(bf16[384,640]{1,0:T(8,128)(2,1)} %get-tuple-element.58), channel_id=1, source_target_pairs={{0,4},{4,0},{8,12},{12,8},{16,20},{20,16},{24,28},{28,24},{1,5},{5... | collective-permute-start | bytes 1474568 | tf_op jit(solution)/shard_map/ppermute | solution.py:333
  168.5 18.0 %copy-start.6 = (bf16[384,1280]{1,0:T(8,128)(2,1)S(1)}, bf16[384,1280]{1,0:T(8,128)(2,1)}, u32[]{:S(2)}) copy-start(bf16[384,1280]{1,0:T(8,128)(2,1)} %get-tuple-element.50) | copy-start | bytes 2949124
  184.9 9.1 %copy-start.8 = (bf16[384,640]{1,0:T(8,128)(2,1)S(1)}, bf16[384,640]{1,0:T(8,128)(2,1)}, u32[]{:S(2)}) copy-start(bf16[384,640]{1,0:T(8,128)(2,1)} %get-tuple-element.57) | copy-start | bytes 1474564
  184.9 9.1 %copy-start.9 = (bf16[384,640]{1,0:T(8,128)(2,1)S(1)}, bf16[384,640]{1,0:T(8,128)(2,1)}, u32[]{:S(2)}) copy-start(bf16[384,640]{1,0:T(8,128)(2,1)} %get-tuple-element.66) | copy-start | bytes 1474564
  184.9 9.1 %collective-permute-start.22 = (bf16[384,640]{1,0:T(8,128)(2,1)}, bf16[384,640]{1,0:T(8,128)(2,1)S(1)}, u32[]{:S(2)}, u32[]{:S(2)}) collective-permute-start(bf16[384,640]{1,0:T(8,128)(2,1)} %get-tuple-element.67), channel_id=1, source_target_pairs={{0,4},{4,0},{8,12},{12,8},{16,20},{20,16},{24,28},{28,24},{1,5},{5... | collective-permute-start | bytes 1474568 | tf_op jit(solution)/shard_map/ppermute | solution.py:333

commit v3 on v2

--- a/solution.py
+++ b/solution.py
@@ -360,7 +360,8 @@
         + neighbour % tiles
     )
     index = jnp.clip(index, 0, 6 * tiles - 1).reshape(-1)
-    v_keep, v_send = mine(v_in), theirs(v_in)
+    v_send = theirs(v_in)
+    v_keep = mine(after(v_in, v_send))
     v_got = partner(v_send)
     v_up, v_down = up(v_keep), down(v_keep)
 
@@ -380,7 +381,7 @@
     order = 2 * shard_text
     relayed = pairs <= 4
     if relayed:
-        text_got = partner(after(theirs(text_both), v_got))
+        text_got = partner(after(theirs(text_both), v_got, got_meta))
         text_pair = jnp.concatenate([mine(text_both), text_got], axis=1)
         start, text_side = (pairs - 1 - pair) * order, side
     else:
@@ -391,44 +392,32 @@
 
     keep_q, keep_k, keep_cq, send_q, send_k, send_cq = pack(
         jnp.reshape(side, (1,)),
-        totals[:, : 3 * tokens].reshape(2, 3, 1, tokens),
+        after(totals[:, : 3 * tokens].reshape(2, 3, 1, tokens), text_got),
         jnp.stack([q_gain, k_gain, cross_q_gain]),
         (q_raw, k_raw, cross_q_raw),
     )
     got_k = partner(after(send_k, text_got, v_up, v_down))
-    got_cq = partner(after(send_cq, got_k, got_meta))
-    got_q = partner(after(send_q, got_cq))
+    got_q = partner(after(send_q, got_k, v_got_up, v_got_down))
+    got_cq = partner(after(send_cq, got_q))
     cross_pieces = [keep_cq, got_cq]
     q_pieces = [keep_q, got_q]
 
     if relayed:
         text_pair = after(text_pair, v_up, v_down)
         ups, downs = [text_pair], [text_pair]
-        for step in range(pairs - 1):
+        for step in range(pairs - 2):
             ups.append(up(ups[-1], step))
             downs.append(down(downs[-1], step))
-        text = ups[:0:-1] + [text_pair] + downs[1:]
-    else:
-        text = [text_got]
     joined_k = join(keep_k, got_k, chunks)
-    k_pieces = []
-    for number, own in enumerate(joined_k):
-        if number == 0:
-            own = after(own, v_got_up, v_got_down)
-        own = after(own, *text[max(0, 1 - number) : len(text) - max(0, 1 - number)])
-        k_pieces.append([up(own), own, down(own)])
-
-    cross_keep, cross_send = cross_attention(place, text, cross_pieces, text_total, order)
-    cross_got = partner(after(cross_send, got_q))
-    self_keep, self_got = [], []
-    calls = [(0, 0, cuts[1]), (1, cuts[1], heads)]
-    for order_of_call, (number, c0, c1) in enumerate(calls):
-        waits = [cross_keep, *self_keep]
-        waits += [cross_got, *self_got][:order_of_call]
+
+    def spread(own):
+        return [up(own), own, down(own)]
+
+    def attend(k_pieces, number, c0, c1, *waits):
         out_keep, out_send = self_attention(
             index,
             count,
-            [after(k, *waits) for k in k_pieces[number]],
+            [after(k, *waits) for k in k_pieces] if waits else k_pieces,
             v_pieces,
             q_pieces,
             c0,
@@ -437,8 +426,29 @@
             tile,
             slots,
         )
-        self_keep.append(out_keep)
-        self_got.append(partner(out_send))
+        return out_keep, partner(out_send)
+
+    text_near = (ups[1], downs[1]) if relayed and pairs > 2 else ()
+    k_first = spread(after(joined_k[0], v_got_up, v_got_down, *text_near))
+    first = attend(k_first, 0, 0, cuts[1])
+    if relayed:
+        if pairs > 1:
+            ups.append(up(after(ups[-1], first[0]), pairs - 2))
+            downs.append(down(after(downs[-1], first[0]), pairs - 2))
+        inner = ups[-2 if pairs > 2 else -1], downs[-2 if pairs > 2 else -1]
+        text = ups[:0:-1] + [text_pair] + downs[1:]
+    else:
+        inner = ()
+        text = [text_got]
+    k_second = spread(after(joined_k[1], first[0], *inner))
+    cross_keep, cross_send = cross_attention(
+        place, text, [after(cross_pieces[0], first[0]), cross_pieces[1]], text_total, order
+    )
+    cross_got = partner(cross_send)
+    split = cuts[1] + (heads - cuts[1] + 1) // 2
+    second = attend(k_second, 1, cuts[1], split, cross_keep, first[1])
+    third = attend(k_second, 1, split, heads, second[0], cross_got)
+    self_keep, self_got = zip(first, second, third)
 
     def joined(own, got):
         rows = jnp.arange(2, dtype=jnp.int32)[:, None, None] == side

time: 197 us -> 198 us (level)
  waiting for transfers between devices: 64.4 us -> 56.1 us
  other arithmetic: 7.04 us -> 12.9 us
  Pallas kernels: 56.7 us -> 59.6 us
    ppermute x7, waiting for transfers between devices: 0.02 us -> 11.1 us  [up(): return lax.ppermute(value, 'frame', moves)]
    ppermute x7, waiting for transfers between devices: 34.9 us -> 24.3 us  [down(): return lax.ppermute(value, 'frame', moves)]
    ppermute x9 -> x10, waiting for transfers between devices: 29.5 us -> 20.7 us  [partner(): return lax.ppermute(value, 'frame', [(i, i ^ 1) for i in range(shards)])]
    reduce_sum x3, other arithmetic: 1.45 us -> 4.57 us  [squares(): return jnp.sum(values * values, axis=-1)]
    pallas_call x2 -> x3, Pallas kernels: 32.5 us -> 35.3 us  [self_attention(): pl.pallas_call(functools.partial(self_kernel, tile=tile, slots=slots, n_k...]
    unnamed x48, local copies, waits for them, and re-layouts: 1.05 us -> 3.39 us
    ppermute x9 -> x10, starting transfers between devices: 11 us -> 13.1 us  [partner(): return lax.ppermute(value, 'frame', [(i, i ^ 1) for i in range(shards)])]
  transfers between devices with their start and end apart: 23 -> 24, of which waited for: 5 -> 11; matrix products, arithmetic and copies ran while one was open for 4% -> 7% of each run, Pallas kernels for 29% -> 26%
where the time goes in v3:
time: 198 us; the launch traced here: 197 us
  Pallas kernels  59.6 us (30%)
  waiting for transfers between devices  56.1 us (28%)
  starting transfers between devices  49.3 us (25%)
  other arithmetic  12.9 us (7%)
  blocking collectives  11 us (6%)
  local copies, waits for them, and re-layouts  7.08 us (4%)
    pallas_call x3, Pallas kernels, self_attention(): pl.pallas_call(functools.partial(self_kernel, tile=tile, slots=slots, n_k...  35.3 us
    ppermute x7, starting transfers between devices, up(): return lax.ppermute(value, 'frame', moves)  27.3 us
    ppermute x7, waiting for transfers between devices, down(): return lax.ppermute(value, 'frame', moves)  24.3 us
    ppermute x10, waiting for transfers between devices, partner(): return lax.ppermute(value, 'frame', [(i, i ^ 1) for i in range(shards)])  20.7 us
    pallas_call x1, Pallas kernels, cross_attention(): pl.pallas_call(functools.partial(cross_kernel, n_text=len(text), text_tot...  13.8 us
    ppermute x10, starting transfers between devices, partner(): return lax.ppermute(value, 'frame', [(i, i ^ 1) for i in range(shards)])  13.1 us
    ppermute x7, waiting for transfers between devices, up(): return lax.ppermute(value, 'frame', moves)  11.1 us
    psum x1, blocking collectives, body(): totals = lax.psum(sums, 'head')  11 us
  transfers between devices with their start and end apart: 24, of which 11 were waited for; matrix products, arithmetic and copies ran while one was open for 7% of the time, Pallas kernels for 26%

profile of v3, /device:TPU:0, one launch (start us, length us, event | category | flops | bytes accessed | tf_op | source)
XLA Modules:
  0.0 197.0 jit_solution(16414399880838970772)
XLA Ops:
  0.7 1.5 copy-done
  2.2 1.0 dynamic-slice_bitcast_fusion.1
  3.2 3.0 %collective-permute-start.1 = (bf16[384,1280]{1,0:T(8,128)(2,1)}, bf16[384,1280]{1,0:T(8,128)(2,1)}, u32[]{:S(2)}, u32[]{:S(2)}) collective-permute-start(bf16[384,1280]{1,0:T(8,128)(2,1)} %dynamic-slice_bitcast_fusion.1), channel_id=1, source_target_pairs={{0,4},{4,0},{8,12},{12,8},{16,20},{20,16},{24,28},{28,24},{1,5},{5... | collective-permute-start | bytes 2949128 | tf_op jit(solution)/shard_map/ppermute | solution.py:333
  6.2 4.6 %collective-permute-start.3 = (bf16[384,1280]{1,0:T(8,128)(2,1)S(1)}, bf16[384,1280]{1,0:T(8,128)(2,1)}, u32[]{:S(2)}, u32[]{:S(2)}) collective-permute-start(bf16[384,1280]{1,0:T(8,128)(2,1)S(1)} %dynamic-slice_bitcast_fusion.refs_5_), channel_id=1, source_target_pairs={{0,8},{4,12},{8,16},{12,20},{16,24},{20,28},{1,9},{5,13},{9,17},{1... | collective-permute-start | bytes 2949128 | tf_op jit(solution)/shard_map/ppermute | solution.py:337
  10.8 1.3 collective-permute-start.4
  12.8 2.0 %multiply_reduce_fusion.2 = f32[2,384]{1,0:T(2,128)S(1)} fusion(bf16[2,384,1280]{2,1,0:T(8,128)(2,1)} %refs_0_.1), kind=kLoop, calls=%fused_computation.2 | loop fusion | flops 2948352 | bytes 1969152 | tf_op jit(solution)/shard_map/reduce_sum | solution.py:25
  15.0 2.4 %multiply_reduce_fusion = (f32[2,384]{1,0:T(2,128)S(1)}, f32[2,384]{1,0:T(2,128)S(1)}) fusion(bf16[2,384,1280]{2,1,0:T(8,128)(2,1)S(1)} %copy-done.1, bf16[2,384,1280]{2,1,0:T(8,128)(2,1)} %refs_1_.1), kind=kLoop, calls=%fused_computation | loop fusion | flops 5896704 | bytes 3938304 | tf_op jit(solution)/shard_map/reduce_sum | solution.py:25
  17.5 11.0 %psum.7 = f32[2,1216]{1,0:T(2,128)S(1)} all-reduce(f32[2,1216]{1,0:T(2,128)S(1)} %pad_maximum_fusion.3), channel_id=1, replica_groups=mesh['frame'=8,'head'=4] {'head'}, use_global_device_ids=true, to_apply=%region_4.5 | all-reduce | flops 2432 | bytes 19456 | tf_op jit(solution)/shard_map/psum | solution.py:372
  28.6 1.8 fusion.2
  30.4 1.5 collective-permute-start.2
  33.1 4.6 %collective-permute-start.6 = (bf16[384,1280]{1,0:T(8,128)(2,1)}, bf16[384,1280]{1,0:T(8,128)(2,1)S(1)}, u32[]{:S(2)}, u32[]{:S(2)}) collective-permute-start(bf16[384,1280]{1,0:T(8,128)(2,1)} %collective-permute-done.1.refs_6_), channel_id=1, source_target_pairs={{0,8},{4,12},{8,16},{12,20},{16,24},{20,28},{1,9},{5,13},{9,17},{1... | collective-permute-start | bytes 2949128 | tf_op jit(solution)/shard_map/ppermute | solution.py:337
  37.7 1.3 collective-permute-start.7
  39.6 7.5 %norm_pack.1 = (bf16[384,1280]{1,0:T(8,128)(2,1)}, bf16[384,1280]{1,0:T(8,128)(2,1)}, bf16[384,1280]{1,0:T(8,128)(2,1)}, bf16[384,1280]{1,0:T(8,128)(2,1)}, bf16...) custom-call(s32[1]{0:T(128)} %bitcast.1.side, f32[2,3,1,384]{3,2,1,0:T(1,128)} %reshape.30.totals, ...), custom_call_target="tpu_custom_call" | custom-call | bytes 1024 | tf_op jit(solution)/shard_map/norm_pack/pallas_call | solution.py:104
  47.1 1.6 collective-permute-start.5
  48.7 1.0 pad_maximum_fusion.1.refs_3_
  49.7 4.6 %collective-permute-start.8 = (bf16[2,128,1280]{2,1,0:T(8,128)(2,1)S(1)}, bf16[2,128,1280]{2,1,0:T(8,128)(2,1)S(1)}, u32[]{:S(2)}, u32[]{:S(2)}) collective-permute-start(bf16[2,128,1280]{2,1,0:T(8,128)(2,1)S(1)} %pad_maximum_fusion.1.refs_3_), channel_id=1, source_target_pairs={{0,8},{4,12},{8,16},{12,20},{16,24},{20,28},{1,9},{5,13},{9,17},{1... | collective-permute-start | bytes 1966088 | tf_op jit(solution)/shard_map/ppermute | solution.py:337
  54.3 1.3 collective-permute-start.9
  55.6 4.6 %collective-permute-done.6.refs_4_ = bf16[384,1280]{1,0:T(8,128)(2,1)S(1)} collective-permute-done((bf16[384,1280]{1,0:T(8,128)(2,1)}, bf16[384,1280]{1,0:T(8,128)(2,1)S(1)}, u32[]{:S(2)}, u32[]{:S(2)}) %collective-permute-start.6) | collective-permute-done | bytes 983072 | tf_op jit(solution)/shard_map/ppermute | solution.py:337
  60.2 4.3 %collective-permute-done.7.refs_8_ = bf16[384,1280]{1,0:T(8,128)(2,1)S(1)} collective-permute-done((bf16[384,1280]{1,0:T(8,128)(2,1)}, bf16[384,1280]{1,0:T(8,128)(2,1)S(1)}, u32[]{:S(2)}, u32[]{:S(2)}) %collective-permute-start.7) | collective-permute-done | bytes 983072 | tf_op jit(solution)/shard_map/ppermute | solution.py:341
  64.5 4.9 %collective-permute-done.5.second = bf16[384,1280]{1,0:T(8,128)(2,1)S(1)} collective-permute-done((bf16[384,1280]{1,0:T(8,128)(2,1)}, bf16[384,1280]{1,0:T(8,128)(2,1)S(1)}, u32[]{:S(2)}, u32[]{:S(2)}) %collective-permute-start.5) | collective-permute-done | bytes 983072 | tf_op jit(solution)/shard_map/ppermute | solution.py:333
  69.4 1.5 collective-permute-start.12
  71.0 2.9 %join.1 = (bf16[768,640]{1,0:T(8,128)(2,1)}, bf16[768,640]{1,0:T(8,128)(2,1)}) custom-call(bf16[384,1280]{1,0:T(8,128)(2,1)} %get-tuple-element.47.first, bf16[384,1280]{1,0:T(8,128)(2,1)} %copy-done.4), custom_call_target="tpu_custom_call" | custom-call | bytes 1024 | tf_op jit(solution)/shard_map/join/pallas_call | solution.py:130
  73.9 2.5 %collective-permute-done.9.refs_4_ = bf16[2,128,1280]{2,1,0:T(8,128)(2,1)} collective-permute-done((bf16[2,128,1280]{2,1,0:T(8,128)(2,1)S(1)}, bf16[2,128,1280]{2,1,0:T(8,128)(2,1)}, u32[]{:S(2)}, u32[]{:S(2)}) %collective-permute-start.9) | collective-permute-done | bytes 655392 | tf_op jit(solution)/shard_map/ppermute | solution.py:341
  76.4 4.2 %collective-permute-start.10 = (bf16[768,640]{1,0:T(8,128)(2,1)}, bf16[768,640]{1,0:T(8,128)(2,1)}, u32[]{:S(2)}, u32[]{:S(2)}) collective-permute-start(bf16[768,640]{1,0:T(8,128)(2,1)} %get-tuple-element.52.refs_1_), channel_id=1, source_target_pairs={{0,8},{4,12},{8,16},{12,20},{16,24},{20,28},{1,9},{5,13},{9,17},{1... | collective-permute-start | bytes 2949128 | tf_op jit(solution)/shard_map/ppermute | solution.py:337
  80.6 1.3 collective-permute-start.11
  83.4 1.3 collective-permute-start.15
  84.6 1.5 collective-permute-start.14
  86.2 5.1 %collective-permute-done.12.refs_10_ = bf16[384,1280]{1,0:T(8,128)(2,1)S(1)} collective-permute-done((bf16[384,1280]{1,0:T(8,128)(2,1)}, bf16[384,1280]{1,0:T(8,128)(2,1)S(1)}, u32[]{:S(2)}, u32[]{:S(2)}) %collective-permute-start.12) | collective-permute-done | bytes 983072 | tf_op jit(solution)/shard_map/ppermute | solution.py:333
  91.3 1.5 collective-permute-start.19
  92.8 6.5 %collective-permute-done.10.refs_0_ = bf16[768,640]{1,0:T(8,128)(2,1)} collective-permute-done((bf16[768,640]{1,0:T(8,128)(2,1)}, bf16[768,640]{1,0:T(8,128)(2,1)}, u32[]{:S(2)}, u32[]{:S(2)}) %collective-permute-start.10) | collective-permute-done | bytes 983072 | tf_op jit(solution)/shard_map/ppermute | solution.py:337
  99.3 8.2 %collective-permute-done.11.refs_2_ = bf16[768,640]{1,0:T(8,128)(2,1)} collective-permute-done((bf16[768,640]{1,0:T(8,128)(2,1)}, bf16[768,640]{1,0:T(8,128)(2,1)}, u32[]{:S(2)}, u32[]{:S(2)}) %collective-permute-start.11) | collective-permute-done | bytes 983072 | tf_op jit(solution)/shard_map/ppermute | solution.py:341
  107.5 16.3 %self_attention.3 = (bf16[384,640]{1,0:T(8,128)(2,1)}, bf16[384,640]{1,0:T(8,128)(2,1)}) custom-call(s32[84]{0:T(128)} %reshape.28.index, s32[6]{0:T(128)} %slice_reduce_fusion.count, bf16[768,640]{1,0:T(8,128)(2,1)} %collective-permute-done.10.refs_0_, bf16[768,640]{1,0:T(8,128)(2,1)} %get-tuple-element.52.refs_1_, ...), custom_call_target="tpu_custom_call" | custom-call | flops 7046430720 | bytes 7864320 | tf_op jit(solution)/shard_map/self_attention/pallas_call | solution.py:200
  123.8 1.3 collective-permute-start.18
  125.1 1.5 collective-permute-start.17
  126.6 1.3 collective-permute-start.20
  127.9 6.2 %collective-permute-start.16 = (bf16[768,640]{1,0:T(8,128)(2,1)}, bf16[768,640]{1,0:T(8,128)(2,1)}, u32[]{:S(2)}, u32[]{:S(2)}) collective-permute-start(bf16[768,640]{1,0:T(8,128)(2,1)} %get-tuple-element.74.refs_1_), channel_id=1, source_target_pairs={{0,8},{4,12},{8,16},{12,20},{16,24},{20,28},{1,9},{5,13},{9,17},{1... | collective-permute-start | bytes 2949128 | tf_op jit(solution)/shard_map/ppermute | solution.py:337
  134.2 9.2 %collective-permute-done.18.refs_6_ = bf16[2,128,1280]{2,1,0:T(8,128)(2,1)S(1)} collective-permute-done((bf16[2,128,1280]{2,1,0:T(8,128)(2,1)S(1)}, bf16[2,128,1280]{2,1,0:T(8,128)(2,1)S(1)}, u32[]{:S(2)}, u32[]{:S(2)}) %collective-permute-start.18) | collective-permute-done | bytes 655392 | tf_op jit(solution)/shard_map/ppermute | solution.py:341
  145.4 1.2 pad_add_fusion.2.place
  146.6 13.8 %cross_attention.1 = (bf16[384,1280]{1,0:T(8,128)(2,1)}, bf16[384,1280]{1,0:T(8,128)(2,1)}) custom-call(s32[3]{0:T(128)} %pad_add_fusion.2.place, bf16[2,128,1280]{2,1,0:T(8,128)(2,1)} %collective-permute-done.17.refs_0_, bf16[2,128,1280]{2,1,0:T(8,128)(2,1)} %collective-permute-done.14.refs_1_, bf16[2,128,1280]{2,1,0:T(8,128)(2,1)} %copy-done.20, ...), custom_call_target="tpu_custom_call" | custom-call | flops 4026531840 | bytes 8519680 | tf_op jit(solution)/shard_map/cross_attention/pallas_call | solution.py:280
  160.4 1.5 collective-permute-start.22
  161.9 0.9 copy-done.9
  162.8 10.8 %self_attention.4 = (bf16[384,384]{1,0:T(8,128)(2,1)}, bf16[384,384]{1,0:T(8,128)(2,1)}) custom-call(s32[84]{0:T(128)} %reshape.28.index, s32[6]{0:T(128)} %slice_reduce_fusion.count, bf16[768,640]{1,0:T(8,128)(2,1)} %collective-permute-done.16.refs_0_, bf16[768,640]{1,0:T(8,128)(2,1)} %get-tuple-element.74.refs_1_, bf16[768,640]{1,0:T(8,128)(2,1)} %copy-done.9, ...), custom_call_target="tpu_custom_call" | custom-call | flops 4227858432 | bytes 4718592 | tf_op jit(solution)/shard_map/self_attention/pallas_call | solution.py:200
  174.5 6.6 %collective-permute-done.21 = bf16[384,384]{1,0:T(8,128)(2,1)S(1)} collective-permute-done((bf16[384,384]{1,0:T(8,128)(2,1)}, bf16[384,384]{1,0:T(8,128)(2,1)S(1)}, u32[]{:S(2)}, u32[]{:S(2)}) %collective-permute-start.21) | collective-permute-done | bytes 294944 | tf_op jit(solution)/shard_map/ppermute | solution.py:333
  181.2 8.3 %self_attention.5 = (bf16[384,256]{1,0:T(8,128)(2,1)}, bf16[384,256]{1,0:T(8,128)(2,1)}) custom-call(s32[84]{0:T(128)} %reshape.28.index, s32[6]{0:T(128)} %slice_reduce_fusion.count, bf16[768,640]{1,0:T(8,128)(2,1)} %collective-permute-done.16.refs_0_, bf16[768,640]{1,0:T(8,128)(2,1)} %get-tuple-element.74.refs_1_, bf16[768,640]{1,0:T(8,128)(2,1)} %copy-done.9, ...), custom_call_target="tpu_custom_call" | custom-call | flops 2818572288 | bytes 3145728 | tf_op jit(solution)/shard_map/self_attention/pallas_call | solution.py:200
  189.5 0.9 collective-permute-start.23
  190.4 1.5 broadcast_select_fusion
  191.9 3.6 %collective-permute-done.23 = bf16[384,256]{1,0:T(8,128)(2,1)S(1)} collective-permute-done((bf16[384,256]{1,0:T(8,128)(2,1)}, bf16[384,256]{1,0:T(8,128)(2,1)S(1)}, u32[]{:S(2)}, u32[]{:S(2)}) %collective-permute-start.23) | collective-permute-done | bytes 196640 | tf_op jit(solution)/shard_map/ppermute | solution.py:333
  195.6 1.4 pad_maximum_fusion
  (85 shorter events, 7.5 us)
Async XLA Ops:
  0.6 1.6 copy-start
  2.2 9.9 %copy-start.19 = (s32[3]{0:T(128)S(1)}, s32[3]{0:T(128)}, u32[]{:S(2)}) copy-start(s32[3]{0:T(128)} %param.24) | copy-start | bytes 40
  2.2 10.0 %copy-start.14 = (s32[3,14]{1,0:T(4,128)S(1)}, s32[3,14]{1,0:T(4,128)}, u32[]{:S(2)}) copy-start(s32[3,14]{1,0:T(4,128)} %param.23) | copy-start | bytes 508
  3.2 27.2 %collective-permute-start.1 = (bf16[384,1280]{1,0:T(8,128)(2,1)}, bf16[384,1280]{1,0:T(8,128)(2,1)}, u32[]{:S(2)}, u32[]{:S(2)}) collective-permute-start(bf16[384,1280]{1,0:T(8,128)(2,1)} %dynamic-slice_bitcast_fusion.1), channel_id=1, source_target_pairs={{0,4},{4,0},{8,12},{12,8},{16,20},{20,16},{24,28},{28,24},{1,5},{5... | collective-permute-start | bytes 2949128 | tf_op jit(solution)/shard_map/ppermute | solution.py:333
  6.2 8.7 %copy-start.3 = (bf16[2,64,1280]{2,1,0:T(8,128)(2,1)S(1)}, bf16[2,64,1280]{2,1,0:T(8,128)(2,1)}, u32[]{:S(2)}) copy-start(bf16[2,64,1280]{2,1,0:T(8,128)(2,1)} %param.17) | copy-start | bytes 983044
  6.2 11.2 %copy-start.2 = (bf16[384,1280]{1,0:T(8,128)(2,1)}, bf16[384,1280]{1,0:T(8,128)(2,1)S(1)}, u32[]{:S(2)}) copy-start(bf16[384,1280]{1,0:T(8,128)(2,1)S(1)} %dynamic-slice_bitcast_fusion.refs_5_) | copy-start | bytes 2949124
  6.2 40.9 %collective-permute-start.3 = (bf16[384,1280]{1,0:T(8,128)(2,1)S(1)}, bf16[384,1280]{1,0:T(8,128)(2,1)}, u32[]{:S(2)}, u32[]{:S(2)}) collective-permute-start(bf16[384,1280]{1,0:T(8,128)(2,1)S(1)} %dynamic-slice_bitcast_fusion.refs_5_), channel_id=1, source_target_pairs={{0,8},{4,12},{8,16},{12,20},{16,24},{20,28},{1,9},{5,13},{9,17},{1... | collective-permute-start | bytes 2949128 | tf_op jit(solution)/shard_map/ppermute | solution.py:337
  10.8 36.3 %collective-permute-start.4 = (bf16[384,1280]{1,0:T(8,128)(2,1)S(1)}, bf16[384,1280]{1,0:T(8,128)(2,1)}, u32[]{:S(2)}, u32[]{:S(2)}) collective-permute-start(bf16[384,1280]{1,0:T(8,128)(2,1)S(1)} %dynamic-slice_bitcast_fusion.refs_5_), channel_id=1, source_target_pairs={{8,0},{12,4},{16,8},{20,12},{24,16},{28,20},{9,1},{13,5},{17,9},{2... | collective-permute-start | bytes 2949128 | tf_op jit(solution)/shard_map/ppermute | solution.py:341
  12.2 2.8 %copy-start.1 = (bf16[2,384,1280]{2,1,0:T(8,128)(2,1)S(1)}, bf16[2,384,1280]{2,1,0:T(8,128)(2,1)}, u32[]{:S(2)}) copy-start(bf16[2,384,1280]{2,1,0:T(8,128)(2,1)} %refs_2_.1) | copy-start | bytes 5898244
  12.3 18.1 %collective-permute-start = (s32[3,15]{1,0:T(4,128)S(1)}, s32[3,15]{1,0:T(4,128)S(1)}, u32[]{:S(2)}, u32[]{:S(2)}) collective-permute-start(s32[3,15]{1,0:T(4,128)S(1)} %pad_add_fusion.1), channel_id=1, source_target_pairs={{0,4},{4,0},{8,12},{12,8},{16,20},{20,16},{24,28},{28,24},{1,5},{5... | collective-permute-start | bytes 548 | tf_op jit(solution)/shard_map/ppermute | solution.py:333
  15.0 13.4 %copy-start.18 = (f32[1280]{0:T(1024)S(1)}, f32[1280]{0:T(1024)}, u32[]{:S(2)}) copy-start(f32[1280]{0:T(1024)} %param.22) | copy-start | bytes 15364
  17.4 15.0 %copy-start.15 = (f32[1280]{0:T(1024)S(1)}, f32[1280]{0:T(1024)}, u32[]{:S(2)}) copy-start(f32[1280]{0:T(1024)} %param.19) | copy-start | bytes 15364
  17.4 15.0 %copy-start.16 = (f32[1280]{0:T(1024)S(1)}, f32[1280]{0:T(1024)}, u32[]{:S(2)}) copy-start(f32[1280]{0:T(1024)} %param.20) | copy-start | bytes 15364
  17.4 15.0 %copy-start.17 = (f32[1280]{0:T(1024)S(1)}, f32[1280]{0:T(1024)}, u32[]{:S(2)}) copy-start(f32[1280]{0:T(1024)} %param.21) | copy-start | bytes 15364
  30.4 9.2 %collective-permute-start.2 = (bf16[2,64,1280]{2,1,0:T(8,128)(2,1)}, bf16[2,64,1280]{2,1,0:T(8,128)(2,1)}, u32[]{:S(2)}, u32[]{:S(2)}) collective-permute-start(bf16[2,64,1280]{2,1,0:T(8,128)(2,1)} %get-tuple-element.45), channel_id=1, source_target_pairs={{0,4},{4,0},{8,12},{12,8},{16,20},{20,16},{24,28},{28,24},{1,5},{5... | collective-permute-start | bytes 983048 | tf_op jit(solution)/shard_map/ppermute | solution.py:333
  33.1 27.1 %collective-permute-start.6 = (bf16[384,1280]{1,0:T(8,128)(2,1)}, bf16[384,1280]{1,0:T(8,128)(2,1)S(1)}, u32[]{:S(2)}, u32[]{:S(2)}) collective-permute-start(bf16[384,1280]{1,0:T(8,128)(2,1)} %collective-permute-done.1.refs_6_), channel_id=1, source_target_pairs={{0,8},{4,12},{8,16},{12,20},{16,24},{20,28},{1,9},{5,13},{9,17},{1... | collective-permute-start | bytes 2949128 | tf_op jit(solution)/shard_map/ppermute | solution.py:337
  37.7 26.8 %collective-permute-start.7 = (bf16[384,1280]{1,0:T(8,128)(2,1)}, bf16[384,1280]{1,0:T(8,128)(2,1)S(1)}, u32[]{:S(2)}, u32[]{:S(2)}) collective-permute-start(bf16[384,1280]{1,0:T(8,128)(2,1)} %collective-permute-done.1.refs_6_), channel_id=1, source_target_pairs={{8,0},{12,4},{16,8},{20,12},{24,16},{28,20},{9,1},{13,5},{17,9},{2... | collective-permute-start | bytes 2949128 | tf_op jit(solution)/shard_map/ppermute | solution.py:341
  47.1 22.3 %collective-permute-start.5 = (bf16[384,1280]{1,0:T(8,128)(2,1)}, bf16[384,1280]{1,0:T(8,128)(2,1)S(1)}, u32[]{:S(2)}, u32[]{:S(2)}) collective-permute-start(bf16[384,1280]{1,0:T(8,128)(2,1)} %get-tuple-element.49), channel_id=1, source_target_pairs={{0,4},{4,0},{8,12},{12,8},{16,20},{20,16},{24,28},{28,24},{1,5},{5... | collective-permute-start | bytes 2949128 | tf_op jit(solution)/shard_map/ppermute | solution.py:333
  49.7 26.7 %copy-start.10 = (bf16[2,128,1280]{2,1,0:T(8,128)(2,1)}, bf16[2,128,1280]{2,1,0:T(8,128)(2,1)S(1)}, u32[]{:S(2)}) copy-start(bf16[2,128,1280]{2,1,0:T(8,128)(2,1)S(1)} %pad_maximum_fusion.1.refs_3_) | copy-start | bytes 1966084
  49.7 24.2 %collective-permute-start.8 = (bf16[2,128,1280]{2,1,0:T(8,128)(2,1)S(1)}, bf16[2,128,1280]{2,1,0:T(8,128)(2,1)S(1)}, u32[]{:S(2)}, u32[]{:S(2)}) collective-permute-start(bf16[2,128,1280]{2,1,0:T(8,128)(2,1)S(1)} %pad_maximum_fusion.1.refs_3_), channel_id=1, source_target_pairs={{0,8},{4,12},{8,16},{12,20},{16,24},{20,28},{1,9},{5,13},{9,17},{1... | collective-permute-start | bytes 1966088 | tf_op jit(solution)/shard_map/ppermute | solution.py:337
  54.3 22.1 %collective-permute-start.9 = (bf16[2,128,1280]{2,1,0:T(8,128)(2,1)S(1)}, bf16[2,128,1280]{2,1,0:T(8,128)(2,1)}, u32[]{:S(2)}, u32[]{:S(2)}) collective-permute-start(bf16[2,128,1280]{2,1,0:T(8,128)(2,1)S(1)} %pad_maximum_fusion.1.refs_3_), channel_id=1, source_target_pairs={{8,0},{12,4},{16,8},{20,12},{24,16},{28,20},{9,1},{13,5},{17,9},{2... | collective-permute-start | bytes 1966088 | tf_op jit(solution)/shard_map/ppermute | solution.py:341
  60.2 13.7 %copy-start.6 = (bf16[384,1280]{1,0:T(8,128)(2,1)}, bf16[384,1280]{1,0:T(8,128)(2,1)S(1)}, u32[]{:S(2)}) copy-start(bf16[384,1280]{1,0:T(8,128)(2,1)S(1)} %collective-permute-done.6.refs_4_) | copy-start | bytes 2949124
  64.5 9.3 %copy-start.7 = (bf16[384,1280]{1,0:T(8,128)(2,1)}, bf16[384,1280]{1,0:T(8,128)(2,1)S(1)}, u32[]{:S(2)}) copy-start(bf16[384,1280]{1,0:T(8,128)(2,1)S(1)} %collective-permute-done.7.refs_8_) | copy-start | bytes 2949124
  69.4 1.5 copy-start.4
  69.4 21.8 %collective-permute-start.12 = (bf16[384,1280]{1,0:T(8,128)(2,1)}, bf16[384,1280]{1,0:T(8,128)(2,1)S(1)}, u32[]{:S(2)}, u32[]{:S(2)}) collective-permute-start(bf16[384,1280]{1,0:T(8,128)(2,1)} %get-tuple-element.55), channel_id=1, source_target_pairs={{0,4},{4,0},{8,12},{12,8},{16,20},{20,16},{24,28},{28,24},{1,5},{5... | collective-permute-start | bytes 2949128 | tf_op jit(solution)/shard_map/ppermute | solution.py:333
  73.9 2.5 %copy-start.20 = (bf16[2,128,1280]{2,1,0:T(8,128)(2,1)}, bf16[2,128,1280]{2,1,0:T(8,128)(2,1)S(1)}, u32[]{:S(2)}) copy-start(bf16[2,128,1280]{2,1,0:T(8,128)(2,1)S(1)} %collective-permute-done.8.refs_2_) | copy-start | bytes 1966084
  76.4 22.9 %collective-permute-start.10 = (bf16[768,640]{1,0:T(8,128)(2,1)}, bf16[768,640]{1,0:T(8,128)(2,1)}, u32[]{:S(2)}, u32[]{:S(2)}) collective-permute-start(bf16[768,640]{1,0:T(8,128)(2,1)} %get-tuple-element.52.refs_1_), channel_id=1, source_target_pairs={{0,8},{4,12},{8,16},{12,20},{16,24},{20,28},{1,9},{5,13},{9,17},{1... | collective-permute-start | bytes 2949128 | tf_op jit(solution)/shard_map/ppermute | solution.py:337
  80.6 26.9 %collective-permute-start.11 = (bf16[768,640]{1,0:T(8,128)(2,1)}, bf16[768,640]{1,0:T(8,128)(2,1)}, u32[]{:S(2)}, u32[]{:S(2)}) collective-permute-start(bf16[768,640]{1,0:T(8,128)(2,1)} %get-tuple-element.52.refs_1_), channel_id=1, source_target_pairs={{8,0},{12,4},{16,8},{20,12},{24,16},{28,20},{9,1},{13,5},{17,9},{2... | collective-permute-start | bytes 2949128 | tf_op jit(solution)/shard_map/ppermute | solution.py:341
  83.4 40.4 %collective-permute-start.15 = (bf16[2,128,1280]{2,1,0:T(8,128)(2,1)}, bf16[2,128,1280]{2,1,0:T(8,128)(2,1)S(1)}, u32[]{:S(2)}, u32[]{:S(2)}) collective-permute-start(bf16[2,128,1280]{2,1,0:T(8,128)(2,1)} %collective-permute-done.9.refs_4_), channel_id=1, source_target_pairs={{8,0},{12,4},{16,8},{20,12},{9,1},{13,5},{17,9},{21,13},{10,2},{14... | collective-permute-start | bytes 1966088 | tf_op jit(solution)/shard_map/ppermute | solution.py:341
  84.6 40.5 %collective-permute-start.14 = (bf16[2,128,1280]{2,1,0:T(8,128)(2,1)}, bf16[2,128,1280]{2,1,0:T(8,128)(2,1)}, u32[]{:S(2)}, u32[]{:S(2)}) collective-permute-start(bf16[2,128,1280]{2,1,0:T(8,128)(2,1)} %copy-done.20), channel_id=1, source_target_pairs={{8,16},{12,20},{16,24},{20,28},{9,17},{13,21},{17,25},{21,29},{10,... | collective-permute-start | bytes 1966088 | tf_op jit(solution)/shard_map/ppermute | solution.py:337
  91.3 16.3 %copy-start.8 = (bf16[384,1280]{1,0:T(8,128)(2,1)}, bf16[384,1280]{1,0:T(8,128)(2,1)S(1)}, u32[]{:S(2)}) copy-start(bf16[384,1280]{1,0:T(8,128)(2,1)S(1)} %collective-permute-done.12.refs_10_) | copy-start | bytes 2949124
  91.3 55.3 %collective-permute-start.19 = (bf16[384,1280]{1,0:T(8,128)(2,1)}, bf16[384,1280]{1,0:T(8,128)(2,1)}, u32[]{:S(2)}, u32[]{:S(2)}) collective-permute-start(bf16[384,1280]{1,0:T(8,128)(2,1)} %get-tuple-element.65), channel_id=1, source_target_pairs={{0,4},{4,0},{8,12},{12,8},{16,20},{20,16},{24,28},{28,24},{1,5},{5... | collective-permute-start | bytes 2949128 | tf_op jit(solution)/shard_map/ppermute | solution.py:333
  107.5 37.3 %copy-start.23 = (s32[2]{0:T(128)S(1)}, s32[2]{0:T(128)}, u32[]{:S(2)}) copy-start(s32[2]{0:T(128)} %param.25) | copy-start | bytes 28
  123.8 19.6 %copy-start.21 = (bf16[2,128,1280]{2,1,0:T(8,128)(2,1)}, bf16[2,128,1280]{2,1,0:T(8,128)(2,1)S(1)}, u32[]{:S(2)}) copy-start(bf16[2,128,1280]{2,1,0:T(8,128)(2,1)S(1)} %collective-permute-done.15.refs_5_) | copy-start | bytes 1966084
  123.8 19.6 %collective-permute-start.18 = (bf16[2,128,1280]{2,1,0:T(8,128)(2,1)S(1)}, bf16[2,128,1280]{2,1,0:T(8,128)(2,1)S(1)}, u32[]{:S(2)}, u32[]{:S(2)}) collective-permute-start(bf16[2,128,1280]{2,1,0:T(8,128)(2,1)S(1)} %collective-permute-done.15.refs_5_), channel_id=1, source_target_pairs={{8,0},{12,4},{9,1},{13,5},{10,2},{14,6},{11,3},{15,7}} | collective-permute-start | bytes 1966088 | tf_op jit(solution)/shard_map/ppermute | solution.py:341
  125.1 21.5 %collective-permute-start.17 = (bf16[2,128,1280]{2,1,0:T(8,128)(2,1)}, bf16[2,128,1280]{2,1,0:T(8,128)(2,1)}, u32[]{:S(2)}, u32[]{:S(2)}) collective-permute-start(bf16[2,128,1280]{2,1,0:T(8,128)(2,1)} %collective-permute-done.14.refs_1_), channel_id=1, source_target_pairs={{16,24},{20,28},{17,25},{21,29},{18,26},{22,30},{19,27},{23,31}} | collective-permute-start | bytes 1966088 | tf_op jit(solution)/shard_map/ppermute | solution.py:337
  126.6 35.2 %collective-permute-start.20 = (bf16[768,640]{1,0:T(8,128)(2,1)}, bf16[768,640]{1,0:T(8,128)(2,1)S(1)}, u32[]{:S(2)}, u32[]{:S(2)}) collective-permute-start(bf16[768,640]{1,0:T(8,128)(2,1)} %get-tuple-element.74.refs_1_), channel_id=1, source_target_pairs={{8,0},{12,4},{16,8},{20,12},{24,16},{28,20},{9,1},{13,5},{17,9},{2... | collective-permute-start | bytes 2949128 | tf_op jit(solution)/shard_map/ppermute | solution.py:341
  127.9 34.0 %collective-permute-start.16 = (bf16[768,640]{1,0:T(8,128)(2,1)}, bf16[768,640]{1,0:T(8,128)(2,1)}, u32[]{:S(2)}, u32[]{:S(2)}) collective-permute-start(bf16[768,640]{1,0:T(8,128)(2,1)} %get-tuple-element.74.refs_1_), channel_id=1, source_target_pairs={{0,8},{4,12},{8,16},{12,20},{16,24},{20,28},{1,9},{5,13},{9,17},{1... | collective-permute-start | bytes 2949128 | tf_op jit(solution)/shard_map/ppermute | solution.py:337
  143.4 0.9 copy-start.22
  144.2 17.7 %collective-permute-start.13 = (bf16[384,640]{1,0:T(8,128)(2,1)}, bf16[384,640]{1,0:T(8,128)(2,1)S(1)}, u32[]{:S(2)}, u32[]{:S(2)}) collective-permute-start(bf16[384,640]{1,0:T(8,128)(2,1)} %get-tuple-element.57), channel_id=1, source_target_pairs={{0,4},{4,0},{8,12},{12,8},{16,20},{20,16},{24,28},{28,24},{1,5},{5... | collective-permute-start | bytes 1474568 | tf_op jit(solution)/shard_map/ppermute | solution.py:333
  160.4 20.8 %collective-permute-start.22 = (bf16[384,1280]{1,0:T(8,128)(2,1)}, bf16[384,1280]{1,0:T(8,128)(2,1)S(1)}, u32[]{:S(2)}, u32[]{:S(2)}) collective-permute-start(bf16[384,1280]{1,0:T(8,128)(2,1)} %get-tuple-element.72), channel_id=1, source_target_pairs={{0,4},{4,0},{8,12},{12,8},{16,20},{20,16},{24,28},{28,24},{1,5},{5... | collective-permute-start | bytes 2949128 | tf_op jit(solution)/shard_map/ppermute | solution.py:333
  161.9 0.9 copy-start.9
  161.9 12.4 %copy-start.11 = (bf16[384,640]{1,0:T(8,128)(2,1)S(1)}, bf16[384,640]{1,0:T(8,128)(2,1)}, u32[]{:S(2)}) copy-start(bf16[384,640]{1,0:T(8,128)(2,1)} %get-tuple-element.56) | copy-start | bytes 1474564
  173.6 7.4 %copy-start.12 = (bf16[384,384]{1,0:T(8,128)(2,1)S(1)}, bf16[384,384]{1,0:T(8,128)(2,1)}, u32[]{:S(2)}) copy-start(bf16[384,384]{1,0:T(8,128)(2,1)} %get-tuple-element.70) | copy-start | bytes 884740
  173.6 7.4 %collective-permute-start.21 = (bf16[384,384]{1,0:T(8,128)(2,1)}, bf16[384,384]{1,0:T(8,128)(2,1)S(1)}, u32[]{:S(2)}, u32[]{:S(2)}) collective-permute-start(bf16[384,384]{1,0:T(8,128)(2,1)} %get-tuple-element.71), channel_id=1, source_target_pairs={{0,4},{4,0},{8,12},{12,8},{16,20},{20,16},{24,28},{28,24},{1,5},{5... | collective-permute-start | bytes 884744 | tf_op jit(solution)/shard_map/ppermute | solution.py:333
  181.2 9.2 %copy-start.5 = (bf16[384,1280]{1,0:T(8,128)(2,1)S(1)}, bf16[384,1280]{1,0:T(8,128)(2,1)}, u32[]{:S(2)}) copy-start(bf16[384,1280]{1,0:T(8,128)(2,1)} %get-tuple-element.66) | copy-start | bytes 2949124
  189.5 6.0 %copy-start.13 = (bf16[384,256]{1,0:T(8,128)(2,1)S(1)}, bf16[384,256]{1,0:T(8,128)(2,1)}, u32[]{:S(2)}) copy-start(bf16[384,256]{1,0:T(8,128)(2,1)} %get-tuple-element.76) | copy-start | bytes 589828
  189.5 5.9 %collective-permute-start.23 = (bf16[384,256]{1,0:T(8,128)(2,1)}, bf16[384,256]{1,0:T(8,128)(2,1)S(1)}, u32[]{:S(2)}, u32[]{:S(2)}) collective-permute-start(bf16[384,256]{1,0:T(8,128)(2,1)} %get-tuple-element.77), channel_id=1, source_target_pairs={{0,4},{4,0},{8,12},{12,8},{16,20},{20,16},{24,28},{28,24},{1,5},{5... | collective-permute-start | bytes 589832 | tf_op jit(solution)/shard_map/ppermute | solution.py:333
